TPU v7x, 32 devices: a whole 2x2x4 slice. The times are simulated.
32 devices in a mesh: bricks: 4 (over y, x), grp: 8 (over z, core).
Axes of the slice: x: 2, y: 2, z: 4, core: 2. Of those that a mesh axis runs over, the one named last changes fastest.
Arguments:
- features: bfloat16 [256, 64, 512], P(('bricks', 'grp')), may hold values from -6 to 6
- occupancy: int32 [256, 512], P(('bricks', 'grp')), may hold values from 0 to 1
- neighbours: int32 [256, 26], P(('bricks', 'grp')), may hold values from -1 to 255, as said below
- coarse_map: int32 [256], P(('bricks', 'grp')), may hold values from 0 to 255, as said below
- norm_gain: float32 [64], replicated, may hold values from 0.1 to 1.9
- time_shift: float32 [64], replicated, may hold values from -4 to 4
- conv_weight: bfloat16 [27, 64, 64], replicated, may hold values from -0.15625 to 0.15625
- stride_weight: bfloat16 [8, 64, 128], replicated, may hold values from -0.25 to 0.25
- coarse_bias: float32 [128], replicated, may hold values from -3 to 3
Outputs:
- fine_out: bfloat16 [256, 64, 512], P(('bricks', 'grp'))
- coarse_out: bfloat16 [32, 128, 512], P(('bricks', 'grp'))
Inputs may be any that keep to these rules, and one draw needn't show every extreme that they name: The key orders bricks by x-slab: brick i lies on device i // 8 of bricks+grp, in the slab of cells with x coordinate i // 8. neighbours[i, o] names the brick at offset o from brick i, or -1 where that cell holds no active brick or lies outside the grid. `coarse_map`: every coarse brick has all eight octants, each named once. Coarse brick c is held by device c // 1. Its eight children lie four on device 2 k and four on device 2 k + 1, with k = c // 2; so each device holds the coarse bricks of exactly 4 of its own bricks, and the coarse bricks of its other 4 bricks are held by the device whose index differs in the lowest bit.
All inputs are finite; a program needn't handle non-finite values.
Results may differ from a plain program's by a relative error of at most 0.0047.
Values may be sent and summed in bfloat16 or wider, within the bound.
A program may use at most 128 MiB of HBM per device.

v0:
```python
import jax
import jax.numpy as jnp
from jax import lax
from jax.sharding import PartitionSpec as P

norm_eps = 1e-06


def padded_2(x, sides, width):
    for axis, dim in sides:
        peers, length = (lax.axis_size(axis), x.shape[dim])
        up = [(i, (i + 1) % peers) for i in range(peers - 1)]
        down = [(j, i) for i, j in up]
        last = lax.slice_in_dim(x, length - width, length, axis=dim)
        initial = lax.slice_in_dim(x, 0, width, axis=dim)
        before = lax.ppermute(last, axis, up)
        after = lax.ppermute(initial, axis, down)
        x = jnp.concatenate([before, x, after], axis=dim)
    return x


def partner(x, axis, bit):
    return lax.ppermute(x, axis, [(i, i ^ 1 << bit) for i in range(lax.axis_size(axis))])


def activate(features, occupancy, norm_gain):
    values = features.astype(jnp.float32)
    scale = lax.rsqrt(jnp.mean(values * values, axis=1, keepdims=True) + norm_eps)
    normed = values * scale * norm_gain[None, :, None]
    mask = occupancy[:, None, :].astype(jnp.float32)
    return (jax.nn.silu(normed) * mask).astype(jnp.bfloat16)


def layer_slice(cubes, axis_pos, shift):
    if shift == -1:
        return lax.slice_in_dim(cubes, 7, 8, axis=axis_pos)
    if shift == 1:
        return lax.slice_in_dim(cubes, 0, 1, axis=axis_pos)
    return cubes


def assemble(center, fetch):
    bricks_here = center.shape[0]
    channels = center.shape[1]
    cube = center.reshape(bricks_here, channels, 8, 8, 8)
    planes = []
    position = 0
    for shift_x in (-1, 0, 1):
        rows_y = []
        for shift_y in (-1, 0, 1):
            cols_z = []
            for shift_z in (-1, 0, 1):
                if shift_x == 0 and shift_y == 0 and (shift_z == 0):
                    cols_z.append(cube)
                else:
                    cols_z.append(fetch(position, shift_x, shift_y, shift_z))
                    position += 1
            rows_y.append(jnp.concatenate(cols_z, axis=4))
        planes.append(jnp.concatenate(rows_y, axis=3))
    return jnp.concatenate(planes, axis=2)


def convolve(padded, conv_weight):
    bricks_here = padded.shape[0]
    channels = padded.shape[1]
    total = jnp.zeros((bricks_here, conv_weight.shape[2], 512), jnp.float32)
    for start_x in range(3):
        for start_y in range(3):
            taps = []
            for start_z in range(3):
                window = padded[
                    :, :, start_x : start_x + 8, start_y : start_y + 8, start_z : start_z + 8
                ]
                taps.append(window.reshape(bricks_here, channels, 512))
            stacked = jnp.concatenate(taps, axis=1)
            first_tap = 9 * start_x + 3 * start_y
            weight = conv_weight[first_tap : first_tap + 3].reshape(3 * channels, -1)
            total = total + jnp.einsum(
                "bcp,cd->bdp", stacked, weight, preferred_element_type=jnp.float32
            )
    return total


def reduce_resolution(fine_features, stride_weight, coarse_bias):
    bricks_here = fine_features.shape[0]
    channels = fine_features.shape[1]
    split = fine_features.reshape(bricks_here, channels, 4, 2, 4, 2, 4, 2)
    kernel = stride_weight.reshape(2, 2, 2, channels, -1)
    octant = jnp.einsum("nciajbkd,abdce->neijk", split, kernel, preferred_element_type=jnp.float32)
    octant = octant + coarse_bias[None, :, None, None, None]
    return octant.reshape(bricks_here, -1).astype(jnp.bfloat16)


def assemble_coarse(placed, coarse_count):
    wide = placed.shape[1] // 64
    shaped = placed.reshape(coarse_count, 2, 2, 2, wide, 4, 4, 4)
    return shaped.transpose(0, 4, 1, 5, 2, 6, 3, 7).reshape(coarse_count, wide, 512)


def shards(
    features,
    occupancy,
    neighbours,
    coarse_map,
    norm_gain,
    time_shift,
    conv_weight,
    stride_weight,
    coarse_bias,
):
    local_count = features.shape[0]
    channels = features.shape[1]
    groups = lax.axis_size("grp")
    device = lax.axis_index("bricks") * groups + lax.axis_index("grp")
    active = activate(features, occupancy, norm_gain)
    cubes = active.reshape(local_count, channels, 8, 8, 8)
    extended = padded_2(active, ((("bricks", "grp"), 0),), local_count)
    lower_face = extended[:local_count].reshape(local_count, channels, 8, 8, 8)[:, :, 7:8]
    upper_face = extended[2 * local_count :].reshape(local_count, channels, 8, 8, 8)[:, :, 0:1]

    def fetch(position, shift_x, shift_y, shift_z):
        target = neighbours[:, position]
        if shift_x == 0:
            source = cubes
            base = device * local_count
        elif shift_x < 0:
            source = lower_face
            base = (device - 1) * local_count
        else:
            source = upper_face
            base = (device + 1) * local_count
        rows = jnp.take(source, jnp.clip(target - base, 0, local_count - 1), axis=0)
        piece = layer_slice(layer_slice(rows, 3, shift_y), 4, shift_z)
        keep = (target >= 0).astype(piece.dtype)
        return piece * keep[:, None, None, None, None]

    padded = assemble(active, fetch)
    conv = convolve(padded, conv_weight)
    summed = features.astype(jnp.float32) + conv + time_shift[None, :, None]
    hidden_state = (occupancy[:, None, :].astype(jnp.float32) * summed).astype(jnp.bfloat16)
    coarse_count = local_count // 8
    half_count = local_count // 2
    coarse_target = coarse_map // 8
    owner_dev = coarse_target // coarse_count
    row_key = coarse_target % coarse_count * 8 + coarse_map % 8
    leaving = (owner_dev != device).astype(jnp.int32)
    order = jnp.argsort(leaving, stable=True)
    stay_rows = order[:half_count]
    go_rows = order[half_count:]
    stay_keys = jnp.take(row_key, stay_rows)
    go_keys = jnp.take(row_key, go_rows)
    sent = jnp.take(hidden_state, go_rows, axis=0)
    arrived, arrived_keys = partner((sent, go_keys), "grp", 0)
    merged_features = jnp.concatenate([jnp.take(hidden_state, stay_rows, axis=0), arrived], axis=0)
    octant_list = reduce_resolution(merged_features, stride_weight, coarse_bias)
    all_keys = jnp.concatenate([stay_keys, arrived_keys], axis=0)
    placed = jnp.zeros_like(octant_list).at[all_keys].set(octant_list)
    return (hidden_state, assemble_coarse(placed, coarse_count))


def solution(mesh):
    return jax.shard_map(
        shards,
        mesh=mesh,
        in_specs=(
            P(("bricks", "grp"), None, None),
            P(("bricks", "grp"), None),
            P(("bricks", "grp"), None),
            P(("bricks", "grp")),
            P(),
            P(),
            P(),
            P(),
            P(),
        ),
        out_specs=(P(("bricks", "grp"), None, None), P(("bricks", "grp"), None, None)),
        check_vma=False,
    )
```

profile of v0, /device:TPU:5, one launch (start us, length us, event | category | flops | bytes accessed | tf_op | source)
XLA Modules:
  0.0 212.3 jit_solution(9912797388509197100)
XLA Ops:
  0.7 1.2 fusion.92
  2.6 2.2 %fusion.100 = bf16[8,64,512]{2,1,0:T(8,128)(2,1)} fusion(bf16[8,64,512]{2,1,0:T(8,128)(2,1)} %param.17, f32[64]{0:T(128)} %param.21, f32[8,512]{1,0:T(8,128)S(1)} %add_rsqrt_fusion, f32[8,512]{1,0:T(8,128)S(1)} %convert_element_type.287), kind=kLoop, calls=%fused_computation.112 | loop fusion | flops 2359296 | bytes 1081600 | tf_op jit(solution)/shard_map/convert_element_type | solution.py:31
  4.9 3.8 %collective-permute-start = (bf16[8,64,512]{2,1,0:T(8,128)(2,1)}, bf16[8,64,512]{2,1,0:T(8,128)(2,1)}, u32[]{:S(2)}, u32[]{:S(2)}) collective-permute-start(bf16[8,64,512]{2,1,0:T(8,128)(2,1)} %fusion.100), channel_id=1, source_target_pairs={{0,1},{1,2},{2,3},{3,4},{4,5},{5,6},{6,7},{7,8},{8,9},{9,10},{10,1... | collective-permute-start | bytes 1572872 | tf_op jit(solution)/shard_map/ppermute | solution.py:16
  8.6 1.9 collective-permute-start.1
  11.9 1.0 sort.17
  14.6 4.1 %collective-permute-start.2 = (s32[4]{0:T(128)}, s32[4]{0:T(128)}, u32[]{:S(2)}, u32[]{:S(2)}) collective-permute-start(s32[4]{0:T(128)} %broadcast_select_fusion.20), channel_id=1, source_target_pairs={{0,1},{1,0},{2,3},{3,2},{4,5},{5,4},{6,7},{7,6},{8,9},{9,8},{10,11... | collective-permute-start | bytes 56 | tf_op jit(solution)/shard_map/ppermute | solution.py:23
  18.8 1.5 copy.128
  38.3 1.8 gather_fusion.16
  40.1 1.6 gather_fusion.15
  41.7 1.8 gather_fusion.14
  45.0 1.7 gather_fusion.11
  46.7 1.7 gather_fusion.10
  48.4 1.7 gather_fusion.9
  56.2 2.5 %pad_maximum_fusion.1 = (bf16[8,64,8,8,8]{1,4,3,2,0:T(8,128)(2,1)}, bf16[8,64,8,8,8]{1,4,3,2,0:T(8,128)(2,1)}) fusion(bf16[8,64,8,8,8]{1,4,3,2,0:T(8,128)(2,1)S(1)} %bitcast.283, bf16[8,64,8,8,1]{1,4,3,2,0:T(2,128)(2,1)S(1)} %fusion.104, bf16[8,64,8,8,1]{1,4,3,2,0:T(2,128)(2,1)S(1)} %fusion.105), kind=kLoop, calls=%fused_computation.114 | loop fusion | flops 2097152 | bytes 1703936 | tf_op jit(solution)/shard_map/concatenate | solution.py:58
  58.7 1.0 fusion.118
  59.7 1.0 fusion.107
  60.7 1.1 fusion.117
  61.8 1.0 fusion.116
  62.8 1.0 fusion.108
  63.9 1.1 fusion.115
  64.9 3.6 %maximum_maximum_fusion.3 = (bf16[8,64,8,9,10]{1,4,3,2,0:T(8,128)(2,1)S(1)}, bf16[8,64,8,9,10]{1,4,3,2,0:T(8,128)(2,1)S(1)}) fusion(bf16[8,64,8,1,1]{1,4,3,2,0:T(2,128)(2,1)S(1)} %fusion.118, bf16[8,64,8,1,8]{1,4,3,2,0:T(8,128)(2,1)S(1)} %fusion.107, bf16[8,64,8,1,1]{1,4,3,2,0:T(2,128)(2,1)S(1)} %fusion.117, bf16[8,64,8,8,1]{1,4,3,2,0:T(2,128)(2,1)S(1)} %fusion.105, ...), kind=kLoop, calls=%fused_computation.34 | loop fusion | flops 8847360 | bytes 2293760 | tf_op jit(solution)/shard_map/concatenate | solution.py:59
  68.6 2.0 fusion.172
  70.7 2.4 %copy.151 = bf16[8,64,512]{2,1,0:T(8,128)(2,1)} copy(bf16[8,64,512]{1,2,0:T(8,128)(2,1)} %bitcast.329) | data formatting | bytes 1048576 | tf_op jit(solution)/shard_map/reshape | solution.py:74
  73.0 2.4 %copy.150 = bf16[8,64,512]{2,1,0:T(8,128)(2,1)} copy(bf16[8,64,512]{1,2,0:T(8,128)(2,1)} %bitcast.327) | data formatting | bytes 1048576 | tf_op jit(solution)/shard_map/reshape | solution.py:74
  75.4 2.3 %copy.149 = bf16[8,64,512]{2,1,0:T(8,128)(2,1)} copy(bf16[8,64,512]{1,2,0:T(8,128)(2,1)} %bitcast.325) | data formatting | bytes 1048576 | tf_op jit(solution)/shard_map/reshape | solution.py:74
  77.7 2.3 %copy.154 = bf16[8,64,512]{2,1,0:T(8,128)(2,1)} copy(bf16[8,64,512]{1,2,0:T(8,128)(2,1)} %bitcast.306) | data formatting | bytes 1048576 | tf_op jit(solution)/shard_map/reshape | solution.py:74
  80.1 2.4 %copy.153 = bf16[8,64,512]{2,1,0:T(8,128)(2,1)} copy(bf16[8,64,512]{1,2,0:T(8,128)(2,1)} %bitcast.305) | data formatting | bytes 1048576 | tf_op jit(solution)/shard_map/reshape | solution.py:74
  82.4 2.0 fusion.171
  84.5 2.5 %copy.158 = bf16[8,64,512]{2,1,0:T(8,128)(2,1)} copy(bf16[8,64,512]{1,2,0:T(8,128)(2,1)} %bitcast.330) | data formatting | bytes 1048576 | tf_op jit(solution)/shard_map/reshape | solution.py:74
  87.0 2.4 %copy.157 = bf16[8,64,512]{2,1,0:T(8,128)(2,1)} copy(bf16[8,64,512]{1,2,0:T(8,128)(2,1)} %bitcast.328) | data formatting | bytes 1048576 | tf_op jit(solution)/shard_map/reshape | solution.py:74
  89.3 1.2 copy.156
  92.6 1.5 copy.118
  99.2 0.8 gather_fusion.1
  107.6 3.4 %maximum_maximum_fusion = bf16[8,64,9,10,10]{1,4,3,2,0:T(8,128)(2,1)S(1)} fusion(bf16[8,64,8,1,1]{1,4,3,2,0:T(2,128)(2,1)S(1)} %copy-done.13, bf16[8,64,8,1,8]{1,4,3,2,0:T(8,128)(2,1)S(1)} %copy-done.8, bf16[8,64,8,1,1]{1,4,3,2,0:T(2,128)(2,1)S(1)} %copy-done.15, bf16[8,64,8,8,1]{1,4,3,2,0:T(2,128)(2,1)S(1)} %copy-done.2, ...), kind=kLoop, calls=%fused_computation.31 | loop fusion | flops 9216000 | bytes 1843200 | tf_op jit(solution)/shard_map/concatenate | solution.py:60
  111.0 3.9 %fusion.170 = (bf16[8,64,8,8,8]{1,4,3,2,0:T(8,128)(2,1)S(1)}, bf16[8,64,8,8,8]{1,4,3,2,0:T(8,128)(2,1)}, bf16[8,64,8,8,8]{1,4,3,2,0:T(8,128)(2,1)}, bf16[8,64,8,...) fusion(bf16[8,64,9,10,10]{1,4,3,2,0:T(8,128)(2,1)S(1)} %maximum, ...), kind=kLoop, calls=%fused_computation.337 | loop fusion | bytes 9437184 | tf_op jit(solution)/shard_map/slice | solution.py:71
  114.9 2.4 %copy.139 = bf16[8,64,512]{2,1,0:T(8,128)(2,1)} copy(bf16[8,64,512]{1,2,0:T(8,128)(2,1)} %bitcast.323) | data formatting | bytes 1048576 | tf_op jit(solution)/shard_map/reshape | solution.py:74
  117.3 2.4 %copy.138 = bf16[8,64,512]{2,1,0:T(8,128)(2,1)} copy(bf16[8,64,512]{1,2,0:T(8,128)(2,1)} %bitcast.321) | data formatting | bytes 1048576 | tf_op jit(solution)/shard_map/reshape | solution.py:74
  119.7 2.3 %copy.137 = bf16[8,64,512]{2,1,0:T(8,128)(2,1)} copy(bf16[8,64,512]{1,2,0:T(8,128)(2,1)} %bitcast.319) | data formatting | bytes 1048576 | tf_op jit(solution)/shard_map/reshape | solution.py:74
  122.0 2.3 %copy.143 = bf16[8,64,512]{2,1,0:T(8,128)(2,1)} copy(bf16[8,64,512]{1,2,0:T(8,128)(2,1)} %bitcast.317) | data formatting | bytes 1048576 | tf_op jit(solution)/shard_map/reshape | solution.py:74
  124.4 2.4 %copy.142 = bf16[8,64,512]{2,1,0:T(8,128)(2,1)} copy(bf16[8,64,512]{1,2,0:T(8,128)(2,1)} %bitcast.315) | data formatting | bytes 1048576 | tf_op jit(solution)/shard_map/reshape | solution.py:74
  126.8 2.3 %copy.141 = bf16[8,64,512]{2,1,0:T(8,128)(2,1)} copy(bf16[8,64,512]{1,2,0:T(8,128)(2,1)} %bitcast.313) | data formatting | bytes 1048576 | tf_op jit(solution)/shard_map/reshape | solution.py:74
  129.1 2.3 %copy.147 = bf16[8,64,512]{2,1,0:T(8,128)(2,1)} copy(bf16[8,64,512]{1,2,0:T(8,128)(2,1)} %bitcast.311) | data formatting | bytes 1048576 | tf_op jit(solution)/shard_map/reshape | solution.py:74
  131.4 2.4 %copy.146 = bf16[8,64,512]{2,1,0:T(8,128)(2,1)} copy(bf16[8,64,512]{1,2,0:T(8,128)(2,1)} %bitcast.309) | data formatting | bytes 1048576 | tf_op jit(solution)/shard_map/reshape | solution.py:74
  133.8 1.2 copy.145
  135.0 1.5 copy.161
  144.0 0.8 fusion.120
  148.5 7.3 %maximum_maximum_fusion.1 = bf16[8,64,9,10,10]{1,4,3,2,0:T(8,128)(2,1)S(1)} fusion(bf16[8,64,1,1,1]{1,4,3,2,0:T(2,128)(2,1)S(1)} %fusion.132, bf16[8,64,1,1,8]{1,4,3,2,0:T(8,128)(2,1)S(1)} %fusion.121, bf16[8,64,1,1,1]{1,4,3,2,0:T(2,128)(2,1)S(1)} %fusion.131, bf16[8,64,1,8,1]{1,4,3,2,0:T(2,128)(2,1)S(1)} %fusion.120, ...), kind=kLoop, calls=%fused_computation.32 | loop fusion | flops 16588800 | bytes 1843200 | tf_op jit(solution)/shard_map/concatenate | solution.py:60
  155.8 3.4 %fusion.169 = (bf16[8,64,8,8,8]{1,4,3,2,0:T(8,128)(2,1)S(1)}, bf16[8,64,8,8,8]{1,4,3,2,0:T(8,128)(2,1)S(1)}, bf16[8,64,8,8,8]{1,4,3,2,0:T(8,128)(2,1)S(1)}, bf16...) fusion(bf16[8,64,9,10,10]{1,4,3,2,0:T(8,128)(2,1)S(1)} %maximum, ...), kind=kLoop, calls=%fused_computation.336 | loop fusion | bytes 9437184 | tf_op jit(solution)/shard_map/slice | solution.py:71
  159.2 2.3 %copy.172 = bf16[8,64,512]{2,1,0:T(8,128)(2,1)} copy(bf16[8,64,512]{1,2,0:T(8,128)(2,1)} %bitcast.324) | data formatting | bytes 1048576 | tf_op jit(solution)/shard_map/reshape | solution.py:74
  161.6 2.4 %copy.171 = bf16[8,64,512]{2,1,0:T(8,128)(2,1)} copy(bf16[8,64,512]{1,2,0:T(8,128)(2,1)} %bitcast.322) | data formatting | bytes 1048576 | tf_op jit(solution)/shard_map/reshape | solution.py:74
  163.9 2.3 %copy.170 = bf16[8,64,512]{2,1,0:T(8,128)(2,1)} copy(bf16[8,64,512]{1,2,0:T(8,128)(2,1)} %bitcast.320) | data formatting | bytes 1048576 | tf_op jit(solution)/shard_map/reshape | solution.py:74
  166.3 2.3 %copy.176 = bf16[8,64,512]{2,1,0:T(8,128)(2,1)} copy(bf16[8,64,512]{1,2,0:T(8,128)(2,1)} %bitcast.318) | data formatting | bytes 1048576 | tf_op jit(solution)/shard_map/reshape | solution.py:74
  168.6 2.3 %copy.175 = bf16[8,64,512]{2,1,0:T(8,128)(2,1)} copy(bf16[8,64,512]{1,2,0:T(8,128)(2,1)} %bitcast.316) | data formatting | bytes 1048576 | tf_op jit(solution)/shard_map/reshape | solution.py:74
  171.0 2.3 %copy.174 = bf16[8,64,512]{2,1,0:T(8,128)(2,1)} copy(bf16[8,64,512]{1,2,0:T(8,128)(2,1)} %bitcast.314) | data formatting | bytes 1048576 | tf_op jit(solution)/shard_map/reshape | solution.py:74
  173.3 1.2 copy.180
  174.5 1.2 copy.179
  175.6 1.1 copy.178
  176.8 1.6 fusion
  181.5 1.5 fusion.69
  190.5 1.9 copy.184
  193.2 1.1 scatter_custom_fusion
  194.3 11.0 %reshape.739 = bf16[1,2,2,2,128,4,4,4]{7,6,5,4,3,2,1,0:T(4,128)(2,1)} reshape(bf16[8,8192]{1,0:T(8,128)(2,1)S(1)} %scatter_custom_fusion) | data formatting | bytes 262144 | tf_op jit(solution)/shard_map/reshape | solution.py:96
  205.4 6.1 %copy.186 = bf16[1,128,2,4,2,4,2,4]{1,7,6,5,4,3,2,0:T(4,128)(2,1)S(1)} copy(bf16[1,128,2,4,2,4,2,4]{7,5,3,1,6,4,2,0:T(4,128)(2,1)} %bitcast.287) | data formatting | bytes 262144 | tf_op jit(solution)/shard_map/transpose | solution.py:97
  211.5 0.8 copy.187
  (322 shorter events, 65.8 us)
Async XLA Ops:
  0.6 189.5 %copy-start = (bf16[8,64,128]{2,1,0:T(8,128)(2,1)S(1)}, bf16[8,64,128]{2,1,0:T(8,128)(2,1)}, u32[]{:S(2)}) copy-start(bf16[8,64,128]{2,1,0:T(8,128)(2,1)} %param.24) | copy-start | bytes 393220
  0.6 19.7 %copy-start.6 = (s32[8,26]{1,0:T(8,128)S(1)}, s32[8,26]{1,0:T(8,128)}, u32[]{:S(2)}) copy-start(s32[8,26]{1,0:T(8,128)} %param.19) | copy-start | bytes 2500
  2.6 12.0 %copy-start.47 = (f32[8,512]{1,0:T(8,128)}, f32[8,512]{1,0:T(8,128)S(1)}, u32[]{:S(2)}) copy-start(f32[8,512]{1,0:T(8,128)S(1)} %convert_element_type.287) | copy-start | bytes 49156
  4.9 87.8 %collective-permute-start = (bf16[8,64,512]{2,1,0:T(8,128)(2,1)}, bf16[8,64,512]{2,1,0:T(8,128)(2,1)}, u32[]{:S(2)}, u32[]{:S(2)}) collective-permute-start(bf16[8,64,512]{2,1,0:T(8,128)(2,1)} %fusion.100), channel_id=1, source_target_pairs={{0,1},{1,2},{2,3},{3,4},{4,5},{5,6},{6,7},{7,8},{8,9},{9,10},{10,1... | collective-permute-start | bytes 1572872 | tf_op jit(solution)/shard_map/ppermute | solution.py:16
  8.6 126.3 %collective-permute-start.1 = (bf16[8,64,512]{2,1,0:T(8,128)(2,1)}, bf16[8,64,512]{2,1,0:T(8,128)(2,1)}, u32[]{:S(2)}, u32[]{:S(2)}) collective-permute-start(bf16[8,64,512]{2,1,0:T(8,128)(2,1)} %fusion.100), channel_id=1, source_target_pairs={{1,0},{2,1},{3,2},{4,3},{5,4},{6,5},{7,6},{8,7},{9,8},{10,9},{11,1... | collective-permute-start | bytes 1572872 | tf_op jit(solution)/shard_map/ppermute | solution.py:17
  14.6 173.1 %collective-permute-start.2 = (s32[4]{0:T(128)}, s32[4]{0:T(128)}, u32[]{:S(2)}, u32[]{:S(2)}) collective-permute-start(s32[4]{0:T(128)} %broadcast_select_fusion.20), channel_id=1, source_target_pairs={{0,1},{1,0},{2,3},{3,2},{4,5},{5,4},{6,7},{7,6},{8,9},{9,8},{10,11... | collective-permute-start | bytes 56 | tf_op jit(solution)/shard_map/ppermute | solution.py:23
  55.7 12.9 %copy-start.1 = (bf16[8,64,8,8,1]{1,4,3,2,0:T(2,128)(2,1)}, bf16[8,64,8,8,1]{1,4,3,2,0:T(2,128)(2,1)S(1)}, u32[]{:S(2)}) copy-start(bf16[8,64,8,8,1]{1,4,3,2,0:T(2,128)(2,1)S(1)} %fusion.105) | copy-start | bytes 196612
  56.2 12.4 %copy-start.3 = (bf16[8,64,8,8,1]{1,4,3,2,0:T(2,128)(2,1)}, bf16[8,64,8,8,1]{1,4,3,2,0:T(2,128)(2,1)S(1)}, u32[]{:S(2)}) copy-start(bf16[8,64,8,8,1]{1,4,3,2,0:T(2,128)(2,1)S(1)} %fusion.104) | copy-start | bytes 196612
  59.7 8.9 %copy-start.12 = (bf16[8,64,8,1,1]{1,4,3,2,0:T(2,128)(2,1)}, bf16[8,64,8,1,1]{1,4,3,2,0:T(2,128)(2,1)S(1)}, u32[]{:S(2)}) copy-start(bf16[8,64,8,1,1]{1,4,3,2,0:T(2,128)(2,1)S(1)} %fusion.118) | copy-start | bytes 24580
  60.7 7.8 %copy-start.7 = (bf16[8,64,8,1,8]{1,4,3,2,0:T(8,128)(2,1)}, bf16[8,64,8,1,8]{1,4,3,2,0:T(8,128)(2,1)S(1)}, u32[]{:S(2)}) copy-start(bf16[8,64,8,1,8]{1,4,3,2,0:T(8,128)(2,1)S(1)} %fusion.107) | copy-start | bytes 196612
  61.8 6.8 %copy-start.14 = (bf16[8,64,8,1,1]{1,4,3,2,0:T(2,128)(2,1)}, bf16[8,64,8,1,1]{1,4,3,2,0:T(2,128)(2,1)S(1)}, u32[]{:S(2)}) copy-start(bf16[8,64,8,1,1]{1,4,3,2,0:T(2,128)(2,1)S(1)} %fusion.117) | copy-start | bytes 24580
  62.8 5.8 %copy-start.16 = (bf16[8,64,8,1,1]{1,4,3,2,0:T(2,128)(2,1)}, bf16[8,64,8,1,1]{1,4,3,2,0:T(2,128)(2,1)S(1)}, u32[]{:S(2)}) copy-start(bf16[8,64,8,1,1]{1,4,3,2,0:T(2,128)(2,1)S(1)} %fusion.116) | copy-start | bytes 24580
  63.9 4.7 %copy-start.9 = (bf16[8,64,8,1,8]{1,4,3,2,0:T(8,128)(2,1)}, bf16[8,64,8,1,8]{1,4,3,2,0:T(8,128)(2,1)S(1)}, u32[]{:S(2)}) copy-start(bf16[8,64,8,1,8]{1,4,3,2,0:T(8,128)(2,1)S(1)} %fusion.108) | copy-start | bytes 196612
  64.9 3.7 %copy-start.18 = (bf16[8,64,8,1,1]{1,4,3,2,0:T(2,128)(2,1)}, bf16[8,64,8,1,1]{1,4,3,2,0:T(2,128)(2,1)S(1)}, u32[]{:S(2)}) copy-start(bf16[8,64,8,1,1]{1,4,3,2,0:T(2,128)(2,1)S(1)} %fusion.115) | copy-start | bytes 24580
  84.4 4.9 %copy-start.5 = (bf16[8,64,8,8,8]{1,4,3,2,0:T(8,128)(2,1)S(1)}, bf16[8,64,8,8,8]{1,4,3,2,0:T(8,128)(2,1)}, u32[]{:S(2)}) copy-start(bf16[8,64,8,8,8]{1,4,3,2,0:T(8,128)(2,1)} %get-tuple-element.86) | copy-start | bytes 1572868
  84.4 6.1 %copy-start.66 = (s32[8]{0:T(128)S(1)}, s32[8]{0:T(128)}, u32[]{:S(2)}) copy-start(s32[8]{0:T(128)} %get-tuple-element.29) | copy-start | bytes 100
  84.4 6.1 %copy-start.65 = (s32[8]{0:T(128)S(1)}, s32[8]{0:T(128)}, u32[]{:S(2)}) copy-start(s32[8]{0:T(128)} %get-tuple-element.152) | copy-start | bytes 100
  84.4 6.1 %copy-start.68 = (s32[8]{0:T(128)S(1)}, s32[8]{0:T(128)}, u32[]{:S(2)}) copy-start(s32[8]{0:T(128)} %get-tuple-element.25) | copy-start | bytes 100
  84.4 6.2 %copy-start.67 = (s32[8]{0:T(128)S(1)}, s32[8]{0:T(128)}, u32[]{:S(2)}) copy-start(s32[8]{0:T(128)} %get-tuple-element.154) | copy-start | bytes 100
  84.4 6.2 %copy-start.70 = (s32[8]{0:T(128)S(1)}, s32[8]{0:T(128)}, u32[]{:S(2)}) copy-start(s32[8]{0:T(128)} %get-tuple-element.21) | copy-start | bytes 100
  84.4 6.2 %copy-start.69 = (s32[8]{0:T(128)S(1)}, s32[8]{0:T(128)}, u32[]{:S(2)}) copy-start(s32[8]{0:T(128)} %get-tuple-element.156) | copy-start | bytes 100
  84.5 6.2 %copy-start.71 = (s32[4]{0:T(128)S(1)}, s32[4]{0:T(128)}, u32[]{:S(2)}) copy-start(s32[4]{0:T(128)} %get-tuple-element.13) | copy-start | bytes 52
  84.5 6.9 %copy-start.72 = (s32[8]{0:T(128)S(1)}, s32[8]{0:T(128)}, u32[]{:S(2)}) copy-start(s32[8]{0:T(128)} %get-tuple-element.17) | copy-start | bytes 100
  84.5 7.4 %copy-start.46 = (bf16[27,64,64]{2,1,0:T(8,128)(2,1)S(1)}, bf16[27,64,64]{2,1,0:T(8,128)(2,1)}, u32[]{:S(2)}) copy-start(bf16[27,64,64]{2,1,0:T(8,128)(2,1)} %param.23) | copy-start | bytes 663556
  99.1 8.5 %copy-start.2 = (bf16[8,64,8,8,1]{1,4,3,2,0:T(2,128)(2,1)S(1)}, bf16[8,64,8,8,1]{1,4,3,2,0:T(2,128)(2,1)}, u32[]{:S(2)}) copy-start(bf16[8,64,8,8,1]{1,4,3,2,0:T(2,128)(2,1)} %copy-done.1) | copy-start | bytes 196612
  99.1 8.5 %copy-start.4 = (bf16[8,64,8,8,1]{1,4,3,2,0:T(2,128)(2,1)S(1)}, bf16[8,64,8,8,1]{1,4,3,2,0:T(2,128)(2,1)}, u32[]{:S(2)}) copy-start(bf16[8,64,8,8,1]{1,4,3,2,0:T(2,128)(2,1)} %copy-done.3) | copy-start | bytes 196612
  99.1 8.5 %copy-start.8 = (bf16[8,64,8,1,8]{1,4,3,2,0:T(8,128)(2,1)S(1)}, bf16[8,64,8,1,8]{1,4,3,2,0:T(8,128)(2,1)}, u32[]{:S(2)}) copy-start(bf16[8,64,8,1,8]{1,4,3,2,0:T(8,128)(2,1)} %copy-done.7) | copy-start | bytes 196612
  99.1 8.5 %copy-start.10 = (bf16[8,64,8,1,8]{1,4,3,2,0:T(8,128)(2,1)S(1)}, bf16[8,64,8,1,8]{1,4,3,2,0:T(8,128)(2,1)}, u32[]{:S(2)}) copy-start(bf16[8,64,8,1,8]{1,4,3,2,0:T(8,128)(2,1)} %copy-done.9) | copy-start | bytes 196612
  99.1 8.5 %copy-start.13 = (bf16[8,64,8,1,1]{1,4,3,2,0:T(2,128)(2,1)S(1)}, bf16[8,64,8,1,1]{1,4,3,2,0:T(2,128)(2,1)}, u32[]{:S(2)}) copy-start(bf16[8,64,8,1,1]{1,4,3,2,0:T(2,128)(2,1)} %copy-done.12) | copy-start | bytes 24580
  99.1 8.5 %copy-start.15 = (bf16[8,64,8,1,1]{1,4,3,2,0:T(2,128)(2,1)S(1)}, bf16[8,64,8,1,1]{1,4,3,2,0:T(2,128)(2,1)}, u32[]{:S(2)}) copy-start(bf16[8,64,8,1,1]{1,4,3,2,0:T(2,128)(2,1)} %copy-done.14) | copy-start | bytes 24580
  99.1 8.5 %copy-start.17 = (bf16[8,64,8,1,1]{1,4,3,2,0:T(2,128)(2,1)S(1)}, bf16[8,64,8,1,1]{1,4,3,2,0:T(2,128)(2,1)}, u32[]{:S(2)}) copy-start(bf16[8,64,8,1,1]{1,4,3,2,0:T(2,128)(2,1)} %copy-done.16) | copy-start | bytes 24580
  99.1 8.5 %copy-start.19 = (bf16[8,64,8,1,1]{1,4,3,2,0:T(2,128)(2,1)S(1)}, bf16[8,64,8,1,1]{1,4,3,2,0:T(2,128)(2,1)}, u32[]{:S(2)}) copy-start(bf16[8,64,8,1,1]{1,4,3,2,0:T(2,128)(2,1)} %copy-done.18) | copy-start | bytes 24580
  140.0 1.8 copy-start.63
  140.0 2.5 %copy-start.56 = (pred[8]{0:T(512)(128)(4,1)S(1)}, pred[8]{0:T(512)(128)(4,1)}, u32[]{:S(2)}) copy-start(pred[8]{0:T(512)(128)(4,1)} %get-tuple-element.149) | copy-start | bytes 28
  140.0 4.0 %copy-start.57 = (pred[8]{0:T(512)(128)(4,1)S(1)}, pred[8]{0:T(512)(128)(4,1)}, u32[]{:S(2)}) copy-start(pred[8]{0:T(512)(128)(4,1)} %get-tuple-element.151) | copy-start | bytes 28
  140.0 4.8 %copy-start.59 = (pred[8]{0:T(512)(128)(4,1)S(1)}, pred[8]{0:T(512)(128)(4,1)}, u32[]{:S(2)}) copy-start(pred[8]{0:T(512)(128)(4,1)} %get-tuple-element.24) | copy-start | bytes 28
  140.0 5.5 %copy-start.58 = (pred[8]{0:T(512)(128)(4,1)S(1)}, pred[8]{0:T(512)(128)(4,1)}, u32[]{:S(2)}) copy-start(pred[8]{0:T(512)(128)(4,1)} %get-tuple-element.153) | copy-start | bytes 28
  140.0 7.0 %copy-start.60 = (pred[8]{0:T(512)(128)(4,1)S(1)}, pred[8]{0:T(512)(128)(4,1)}, u32[]{:S(2)}) copy-start(pred[8]{0:T(512)(128)(4,1)} %get-tuple-element.155) | copy-start | bytes 28
  140.6 2.6 %copy-start.64 = (pred[8]{0:T(512)(128)(4,1)S(1)}, pred[8]{0:T(512)(128)(4,1)}, u32[]{:S(2)}) copy-start(pred[8]{0:T(512)(128)(4,1)} %get-tuple-element.28) | copy-start | bytes 28
  171.0 5.8 %copy-start.55 = (bf16[3,64,64]{2,1,0:T(8,128)(2,1)S(1)}, bf16[3,64,64]{2,1,0:T(8,128)(2,1)}, u32[]{:S(2)}) copy-start(bf16[3,64,64]{2,1,0:T(8,128)(2,1)} %get-tuple-element.103) | copy-start | bytes 73732
  174.5 2.3 %copy-start.28 = (bf16[8,64,512]{2,1,0:T(8,128)(2,1)S(1)}, bf16[8,64,512]{2,1,0:T(8,128)(2,1)}, u32[]{:S(2)}) copy-start(bf16[8,64,512]{2,1,0:T(8,128)(2,1)} %copy.139) | copy-start | bytes 1572868
  174.5 2.3 %copy-start.29 = (bf16[8,64,512]{2,1,0:T(8,128)(2,1)S(1)}, bf16[8,64,512]{2,1,0:T(8,128)(2,1)}, u32[]{:S(2)}) copy-start(bf16[8,64,512]{2,1,0:T(8,128)(2,1)} %copy.138) | copy-start | bytes 1572868
  175.6 2.8 %copy-start.30 = (bf16[8,64,512]{2,1,0:T(8,128)(2,1)S(1)}, bf16[8,64,512]{2,1,0:T(8,128)(2,1)}, u32[]{:S(2)}) copy-start(bf16[8,64,512]{2,1,0:T(8,128)(2,1)} %copy.143) | copy-start | bytes 1572868
  175.6 2.8 %copy-start.32 = (bf16[8,64,512]{2,1,0:T(8,128)(2,1)S(1)}, bf16[8,64,512]{2,1,0:T(8,128)(2,1)}, u32[]{:S(2)}) copy-start(bf16[8,64,512]{2,1,0:T(8,128)(2,1)} %copy.142) | copy-start | bytes 1572868
  175.6 2.8 %copy-start.54 = (bf16[3,64,64]{2,1,0:T(8,128)(2,1)S(1)}, bf16[3,64,64]{2,1,0:T(8,128)(2,1)}, u32[]{:S(2)}) copy-start(bf16[3,64,64]{2,1,0:T(8,128)(2,1)} %get-tuple-element.102) | copy-start | bytes 73732
  176.8 1.7 copy-start.34
  179.0 1.5 copy-start.24
  179.0 1.5 copy-start.52
  180.9 2.1 copy-start.25
  180.9 2.1 copy-start.26
  180.9 2.1 copy-start.27
  180.9 2.1 copy-start.50
  183.5 1.4 copy-start.39
  183.5 1.4 copy-start.41
  183.6 1.5 copy-start.44
  184.8 1.4 copy-start.37
  184.9 1.5 copy-start.42
  184.9 1.5 copy-start.48
  184.9 1.5 copy-start.74
  186.4 1.4 copy-start.75
  186.4 2.7 %copy-start.61 = (pred[4]{0:T(512)(128)(4,1)S(1)}, pred[4]{0:T(512)(128)(4,1)}, u32[]{:S(2)}) copy-start(pred[4]{0:T(512)(128)(4,1)} %get-tuple-element.12) | copy-start | bytes 16
  187.0 2.3 %copy-start.45 = (bf16[8,64,512]{2,1,0:T(8,128)(2,1)}, bf16[8,64,512]{2,1,0:T(8,128)(2,1)S(1)}, u32[]{:S(2)}) copy-start(bf16[8,64,512]{2,1,0:T(8,128)(2,1)S(1)} %fusion.89) | copy-start | bytes 1572868
  187.0 3.5 %copy-start.73 = (f32[128]{0:T(128)S(1)}, f32[128]{0:T(128)}, u32[]{:S(2)}) copy-start(f32[128]{0:T(128)} %param.25) | copy-start | bytes 1540
  187.7 1.6 collective-permute-start.3
  (16 other events, 19.6 us)
where the time goes:
time: 214 us; the launch traced here: 212 us
  local copies, waits for them, and re-layouts  126 us (59%)
  other arithmetic  67.3 us (31%)
  starting transfers between devices  9.9 us (5%)
  matrix products  6.88 us (3%)
  between operations  2.23 us (1%)
    reshape x26, local copies, waits for them, and re-layouts, convolve(): taps.append(window.reshape(bricks_here, channels, 512))  55.4 us
    gather x26, local copies, waits for them, and re-layouts, fetch(): rows = jnp.take(source, jnp.clip(target - base, 0, local_count - 1), axis=0)  23.2 us
    mul x26, other arithmetic, fetch(): return piece * keep[:, None, None, None, None]  20 us
    slice x4, local copies, waits for them, and re-layouts, convolve(): padded[:, :, start_x:start_x + 8, start_y:start_y + 8, start_z:start_z + 8]  11.4 us
    reshape x1, local copies, waits for them, and re-layouts, assemble_coarse(): shaped = placed.reshape(coarse_count, 2, 2, 2, wide, 4, 4, 4)  11 us
    concatenate x2, other arithmetic, assemble(): return jnp.concatenate(planes, axis=2)  10.7 us
    convert_element_type x26, other arithmetic, fetch(): keep = (target >= 0).astype(piece.dtype)  9.83 us
    dot_general x9, matrix products, convolve(): jnp.einsum('bcp,cd->bdp', stacked, weight, preferred_element_type=jnp.flo...  6.5 us
  transfers between devices with their start and end apart: 4, of which 1 were waited for; matrix products, arithmetic and copies ran while one was open for 80% of the time, Pallas kernels for 0%

commit v1 on v0

v1 whole, which is shorter than its diff:
```python
import functools

import jax
import jax.numpy as jnp
import numpy as np
from jax import lax
from jax.experimental import pallas as pl
from jax.experimental.pallas import tpu as pltpu
from jax.sharding import PartitionSpec as P

norm_eps = 1e-06
AXES = ("bricks", "grp")
SHIFTS = [(b, c) for b in (-1, 0, 1) for c in (-1, 0, 1)]


def window_matrix():
    table = np.zeros((4, 2, 64, 9, 2, 64), np.float32)
    for w, (b, c) in enumerate(SHIFTS):
        for y in range(8):
            for z in range(8):
                yy, zz = y + b, z + c
                kind = (1 if not 0 <= yy < 8 else 0) + (2 if not 0 <= zz < 8 else 0)
                for half in range(2):
                    table[kind, half, (yy % 8) * 8 + zz % 8, w, half, y * 8 + z] = 1.0
    return table.reshape(512, 1152).astype(jnp.bfloat16)


def stride_matrix():
    table = np.zeros((512, 512), np.float32)
    for x in range(8):
        for y in range(8):
            for z in range(8):
                tap = 4 * (x % 2) + 2 * (y % 2) + z % 2
                place = 16 * (x // 2) + 4 * (y // 2) + z // 2
                table[64 * x + 8 * y + z, 64 * tap + place] = 1.0
    return table.astype(jnp.bfloat16)


def activate(features, occupancy, norm_gain):
    values = features.astype(jnp.float32)
    scale = lax.rsqrt(jnp.mean(values * values, axis=1, keepdims=True) + norm_eps)
    normed = values * scale * norm_gain[None, :, None]
    mask = occupancy[:, None, :].astype(jnp.float32)
    return (jax.nn.silu(normed) * mask).astype(jnp.bfloat16)


def column(row):
    n = row.shape[1]
    at = lax.broadcasted_iota(jnp.int32, (n, n), 0)
    to = lax.broadcasted_iota(jnp.int32, (n, n), 1)
    return jnp.sum(jnp.where(at == to, row, 0.0), axis=1, keepdims=True)


def offset(dx, dy, dz):
    o = 9 * (dx + 1) + 3 * (dy + 1) + dz + 1
    return o - 1 if o > 13 else o


def dot(a, b):
    return jnp.dot(a, b, preferred_element_type=jnp.float32)


def halos(fetch, masks):
    low_y, low_z = masks
    high_y, high_z = 1 - low_y, 1 - low_z
    halo_y = fetch(1, 0) * low_y + fetch(-1, 0) * high_y
    halo_z = fetch(0, 1) * low_z + fetch(0, -1) * high_z
    near = fetch(1, 1) * low_z + fetch(1, -1) * high_z
    far = fetch(-1, 1) * low_z + fetch(-1, -1) * high_z
    return halo_y, halo_z, near * low_y + far * high_y


def fine_kernel(
    near_ref, feat_ref, occ_ref, before_ref, after_ref, gain_ref, shift_ref, bias_ref,
    weight_ref, stride_ref, window_ref, perm_ref,
    fine_ref, oct_ref,
    act, lower, upper,
):
    count = feat_ref.shape[0]
    device = lax.axis_index("bricks") * lax.axis_size("grp") + lax.axis_index("grp")
    gain = column(gain_ref[...])
    shift = column(shift_ref[...])
    bias = column(bias_ref[...])

    def activate_one(i, carry):
        values = feat_ref[i].astype(jnp.float32)
        scale = lax.rsqrt(jnp.mean(values * values, axis=0, keepdims=True) + norm_eps)
        normed = values * scale * gain
        mask = occ_ref[pl.ds(i, 1), :].astype(jnp.float32)
        act[i] = (normed / (1.0 + jnp.exp(-normed)) * mask).astype(jnp.bfloat16)
        return carry

    lax.fori_loop(0, count, activate_one, 0)
    act[count] = jnp.zeros((64, 512), jnp.bfloat16)
    lower[0:count] = before_ref[...]
    upper[0:count] = after_ref[...]
    lower[count] = jnp.zeros((64, 128), jnp.bfloat16)
    upper[count] = jnp.zeros((64, 128), jnp.bfloat16)

    lane = lax.broadcasted_iota(jnp.int32, (64, 512), 1)
    low_y = jnp.where(lane % 64 < 32, 1.0, 0.0).astype(jnp.bfloat16)
    low_z = jnp.where(lane % 8 < 4, 1.0, 0.0).astype(jnp.bfloat16)
    half = lax.broadcasted_iota(jnp.int32, (64, 128), 1) < 64
    first = jnp.where(half, 1.0, 0.0).astype(jnp.bfloat16)
    second = 1 - first

    def brick(i, carry):
        def row(dx, dy, dz):
            target = near_ref[i, offset(dx, dy, dz)]
            local = jnp.clip(target - (device + dx) * count, 0, count - 1)
            return jnp.where(target < 0, count, local)

        def own(dy, dz):
            return act[row(0, dy, dz)]

        def outer(dy, dz):
            return upper[row(1, dy, dz)] * first + lower[row(-1, dy, dz)] * second

        middle = (act[i],) + halos(own, (low_y, low_z))
        edge = (outer(0, 0),) + halos(outer, (low_y[:, :128], low_z[:, :128]))
        rows = [
            jnp.concatenate([m[:, 128 * p : 128 * p + 128] for m in middle], axis=1)
            for p in range(4)
        ]
        rows.append(jnp.concatenate(edge, axis=1))
        windows = dot(jnp.concatenate(rows, axis=0), window_ref[...]).astype(jnp.bfloat16)
        stacked = jnp.concatenate(
            [
                jnp.concatenate(
                    [windows[64 * p : 64 * p + 64, 128 * w : 128 * w + 128] for w in range(9)],
                    axis=0,
                )
                for p in range(5)
            ],
            axis=1,
        )
        product = dot(weight_ref[...], stacked)

        def part(dx, p):
            p = p % 5
            return product[64 * (dx + 1) : 64 * (dx + 2), 128 * p : 128 * p + 128]

        pieces = []
        for p in range(4):
            below = pltpu.roll(jnp.where(half, part(-1, p), part(-1, p - 1)), 64, 1)
            above = pltpu.roll(jnp.where(half, part(1, p + 1), part(1, p)), 64, 1)
            pieces.append(part(0, p) + below + above)
        conv = jnp.concatenate(pieces, axis=1)
        mask = occ_ref[pl.ds(i, 1), :].astype(jnp.float32)
        summed = feat_ref[i].astype(jnp.float32) + conv + shift
        fine_ref[i] = (mask * summed).astype(jnp.bfloat16)
        return carry

    lax.fori_loop(0, count, brick, 0)

    sorted_ = dot(fine_ref[...].reshape(count * 64, 512), perm_ref[...])
    columns = []
    for j in range(0, count, 2):
        taps = []
        for s in range(4):
            one = sorted_[64 * j : 64 * j + 64, 128 * s : 128 * s + 128]
            two = sorted_[64 * j + 64 : 64 * j + 128, 128 * s : 128 * s + 128]
            taps.append(jnp.where(half, one, pltpu.roll(two, 64, 1)))
            taps.append(jnp.where(half, pltpu.roll(one, 64, 1), two))
        columns.append(jnp.concatenate(taps, axis=0).astype(jnp.bfloat16))
    octants = dot(stride_ref[...], jnp.concatenate(columns, axis=1)) + bias
    oct_ref[...] = octants.astype(jnp.bfloat16)


def place(map_ref, octants, coarse, count):
    k = lax.broadcasted_iota(jnp.int32, (64, 512), 0)
    lane = lax.broadcasted_iota(jnp.int32, (64, 512), 1)
    rest = lane - (64 * (k // 16) + 8 * (k // 4 % 4) + k % 4)
    blocks = []
    for j in range(count):
        key = map_ref[j]
        o = key % 8
        start = 256 * (o // 4) + 32 * (o // 2 % 2) + 4 * (o % 2)
        start = jnp.where(key // 8 == coarse, start, -1024)
        blocks.append(jnp.where(rest == start, 1.0, 0.0).astype(jnp.bfloat16))
    return dot(octants, jnp.concatenate(blocks, axis=0))


def coarse_kernel(map_ref, other_ref, oct_ref, came_ref, out_ref):
    count = map_ref.shape[0]
    device = lax.axis_index("bricks") * lax.axis_size("grp") + lax.axis_index("grp")
    total = place(map_ref, oct_ref[...], device, count)
    total = total + place(other_ref, came_ref[...], device, count)
    out_ref[0] = total.astype(jnp.bfloat16)


def partner(x):
    return lax.ppermute(x, "grp", [(i, i ^ 1) for i in range(lax.axis_size("grp"))])


def shards(
    features, occupancy, neighbours, coarse_map, norm_gain, time_shift, conv_weight,
    stride_weight, coarse_bias,
):
    count = features.shape[0]
    peers = lax.axis_size(AXES)
    up = [(i, i + 1) for i in range(peers - 1)]
    down = [(j, i) for i, j in up]
    last = activate(features[:, :, 384:], occupancy[:, 384:], norm_gain)
    first = activate(features[:, :, :128], occupancy[:, :128], norm_gain)
    before = lax.ppermute(last, AXES, up)
    after = lax.ppermute(first, AXES, down)
    other_map = partner(coarse_map)
    weight = conv_weight.reshape(3, 576, 64).transpose(0, 2, 1).reshape(192, 576)
    stride = stride_weight.reshape(512, 128).T
    vmem = pl.BlockSpec(memory_space=pltpu.VMEM)
    smem = pl.BlockSpec(memory_space=pltpu.SMEM)
    params = pltpu.CompilerParams(vmem_limit_bytes=48 * 1024 * 1024)
    fine, octants = pl.pallas_call(
        fine_kernel,
        out_shape=(
            jax.ShapeDtypeStruct(features.shape, jnp.bfloat16),
            jax.ShapeDtypeStruct((128, 64 * count), jnp.bfloat16),
        ),
        in_specs=[smem] + [vmem] * 11,
        out_specs=(vmem, vmem),
        scratch_shapes=[
            pltpu.VMEM((count + 1, 64, 512), jnp.bfloat16),
            pltpu.VMEM((count + 1, 64, 128), jnp.bfloat16),
            pltpu.VMEM((count + 1, 64, 128), jnp.bfloat16),
        ],
        compiler_params=params,
        name="fine",
    )(
        neighbours, features, occupancy, before, after, norm_gain[None], time_shift[None],
        coarse_bias[None], weight, stride, window_matrix(), stride_matrix(),
    )
    came = partner(octants)
    coarse = pl.pallas_call(
        coarse_kernel,
        out_shape=jax.ShapeDtypeStruct((1, 128, 512), jnp.bfloat16),
        in_specs=[smem, smem, vmem, vmem],
        out_specs=vmem,
        compiler_params=params,
        name="coarse",
    )(coarse_map, other_map, octants, came)
    return fine, coarse


def solution(mesh):
    wide = P(AXES, None, None)
    return jax.shard_map(
        shards,
        mesh=mesh,
        in_specs=(wide, P(AXES, None), P(AXES, None), P(AXES), P(), P(), P(), P(), P()),
        out_specs=(wide, wide),
        check_vma=False,
    )
```

time: 214 us -> 32.1 us (0.15)
  the two profiles are of different devices: /device:TPU:5 before, /device:TPU:27 now
where the time goes in v1:
time: 32.1 us; the launch traced here: 31.8 us
  Pallas kernels  12.2 us (38%)
  waiting for transfers between devices  6.55 us (20%)
  starting transfers between devices  5.78 us (18%)
  local copies, waits for them, and re-layouts  3.3 us (10%)
  other arithmetic  3.11 us (10%)
  between operations  0.79 us (2%)
    pallas_call x1, Pallas kernels, shards(): pl.pallas_call(fine_kernel, out_shape=(jax.ShapeDtypeStruct(features.shap...  10.6 us
    ppermute x1, waiting for transfers between devices, shards(): after = lax.ppermute(first, AXES, down)  5.71 us
    ppermute x1, starting transfers between devices, shards(): before = lax.ppermute(last, AXES, up)  3.34 us
    ppermute x1, starting transfers between devices, shards(): after = lax.ppermute(first, AXES, down)  1.92 us
    pallas_call x1, Pallas kernels, shards(): pl.pallas_call(coarse_kernel, out_shape=jax.ShapeDtypeStruct((1, 128, 512...  1.67 us
    convert_element_type x1, other arithmetic, activate(): return (jax.nn.silu(normed) * mask).astype(jnp.bfloat16)  1.24 us
    reshape x1, local copies, waits for them, and re-layouts, shards(): conv_weight.reshape(3, 576, 64).transpose(0, 2, 1).reshape(192, 576)  1.22 us
    reduce_sum x1, other arithmetic, activate(): jnp.mean(values * values, axis=1, keepdims=True) + norm_eps  1.15 us
  transfers between devices with their start and end apart: 4, of which 2 were waited for; matrix products, arithmetic and copies ran while one was open for 7% of the time, Pallas kernels for 0%

profile of v1, /device:TPU:27, one launch (start us, length us, event | category | flops | bytes accessed | tf_op | source)
XLA Modules:
  0.0 31.8 jit_solution(8924205702863042148)
XLA Ops:
  0.6 0.0 copy-start.1
  0.6 0.0 copy-start
  0.7 0.0 copy-start.3
  0.7 0.0 copy-start.5
  0.7 0.0 copy-start.6
  0.7 0.0 copy-start.7
  0.7 0.0 copy-start.4
  0.7 1.2 %fusion.9 = (f32[8,128]{1,0:T(8,128)S(1)}, f32[8,128]{1,0:T(8,128)S(1)}) fusion(bf16[8,64,512]{2,1,0:T(8,128)(2,1)} %feat_ref.1), kind=kLoop, calls=%fused_computation.13 | loop fusion | flops 391168 | bytes 270336 | tf_op jit(solution)/shard_map/reduce_sum | solution.py:41
  1.9 0.7 %slice_convert_fusion = (f32[8,128]{1,0:T(8,128)S(1)}, f32[8,128]{1,0:T(8,128)S(1)}) fusion(s32[8,512]{1,0:T(8,128)} %occ_ref.1), kind=kLoop, calls=%fused_computation.22 | loop fusion | flops 2048 | bytes 16384 | tf_op jit(solution)/shard_map/convert_element_type | solution.py:43
  2.6 1.2 %fusion.17 = (bf16[8,64,128]{2,1,0:T(8,128)(2,1)S(1)}, bf16[8,64,128]{2,1,0:T(8,128)(2,1)S(1)}) fusion(f32[8,128]{1,0:T(8,128)S(1)} %get-tuple-element.10, f32[8,128]{1,0:T(8,128)S(1)} %get-tuple-element.12, f32[64]{0:T(128)} %param.15, bf16[8,64,512]{2,1,0:T(8,128)(2,1)} %feat_ref.1, f32[8,128]{1,0:T(8,128)S(1)} %get-tuple-element.11, ...), kind=kLoop, calls=%fused_computation.21 | loop fusion | flops 1179648 | bytes 540928 | tf_op jit(solution)/shard_map/convert_element_type | solution.py:44
  3.8 3.3 %collective-permute-start = (bf16[8,64,128]{2,1,0:T(8,128)(2,1)S(1)}, bf16[8,64,128]{2,1,0:T(8,128)(2,1)S(1)}, u32[]{:S(2)}, u32[]{:S(2)}) collective-permute-start(bf16[8,64,128]{2,1,0:T(8,128)(2,1)S(1)} %get-tuple-element.9), channel_id=1, source_target_pairs={{0,1},{1,2},{2,3},{3,4},{4,5},{5,6},{6,7},{7,8},{8,9},{9,10},{10,1... | collective-permute-start | bytes 393224 | tf_op jit(solution)/shard_map/ppermute | solution.py:206
  7.2 1.9 %collective-permute-start.1 = (bf16[8,64,128]{2,1,0:T(8,128)(2,1)S(1)}, bf16[8,64,128]{2,1,0:T(8,128)(2,1)S(1)}, u32[]{:S(2)}, u32[]{:S(2)}) collective-permute-start(bf16[8,64,128]{2,1,0:T(8,128)(2,1)S(1)} %get-tuple-element.8), channel_id=1, source_target_pairs={{1,0},{2,1},{3,2},{4,3},{5,4},{6,5},{7,6},{8,7},{9,8},{10,9},{11,1... | collective-permute-start | bytes 393224 | tf_op jit(solution)/shard_map/ppermute | solution.py:207
  9.1 1.2 %copy.15 = bf16[3,576,64]{1,2,0:T(8,128)(2,1)S(1)} copy(bf16[3,576,64]{2,1,0:T(8,128)(2,1)} %bitcast.14) | data formatting | bytes 442368 | tf_op jit(solution)/shard_map/reshape | solution.py:209
  10.3 1.0 %copy.16 = bf16[512,128]{0,1:T(8,128)(2,1)S(1)} copy(bf16[512,128]{1,0:T(8,128)(2,1)} %bitcast.15) | data formatting | bytes 262144 | tf_op jit(solution)/shard_map/reshape | solution.py:210
  11.3 0.0 collective-permute-done.before_ref
  11.3 5.7 %collective-permute-done.1.after_ref = bf16[8,64,128]{2,1,0:T(8,128)(2,1)S(1)} collective-permute-done((bf16[8,64,128]{2,1,0:T(8,128)(2,1)S(1)}, bf16[8,64,128]{2,1,0:T(8,128)(2,1)S(1)}, u32[]{:S(2)}, u32[]{:S(2)}) %collective-permute-start.1) | collective-permute-done | bytes 131104 | tf_op jit(solution)/shard_map/ppermute | solution.py:207
  17.1 0.0 copy-done.1
  17.1 0.0 copy-done
  17.1 0.0 copy-done.3
  17.1 0.0 copy-done.5
  17.1 0.0 copy-done.6
  17.1 0.0 copy-done.7
  17.1 0.0 copy-done.4
  17.1 0.0 copy-start.2
  17.1 1.0 %copy-done.2 = bf16[512,512]{1,0:T(8,128)(2,1)S(1)} copy-done((bf16[512,512]{1,0:T(8,128)(2,1)S(1)}, bf16[512,512]{1,0:T(8,128)(2,1)}, u32[]{:S(2)}) %copy-start.2) | copy-done | bytes 524312
  18.1 0.0 copy-start.8
  18.2 10.6 %fine.1 = (bf16[8,64,512]{2,1,0:T(8,128)(2,1)}, bf16[128,512]{1,0:T(8,128)(2,1)S(1)}) custom-call(s32[8,26]{1,0:T(8,128)S(1)} %copy-done.4, bf16[8,64,512]{2,1,0:T(8,128)(2,1)S(1)} %copy-done, s32[8,512]{1,0:T(8,128)S(1)} %copy-done.3, bf16[8,64,128]{2,1,0:T(8,128)(2,1)S(1)} %collective-permute-done.before_ref, ...), custom_call_target="tpu_custom_call" | custom-call | tf_op jit(solution)/shard_map/fine/pallas_call | solution.py:214
  28.7 0.0 collective-permute-start.3
  28.7 0.0 copy-done.8
  28.8 0.5 %collective-permute-start.2 = (s32[8]{0:T(128)S(1)}, s32[8]{0:T(128)S(1)}, u32[]{:S(2)}, u32[]{:S(2)}) collective-permute-start(s32[8]{0:T(128)S(1)} %copy-done.8), channel_id=1, source_target_pairs={{0,1},{1,0},{2,3},{3,2},{4,5},{5,4},{6,7},{7,6},{8,9},{9,8},{10,11... | collective-permute-start | bytes 104 | tf_op jit(solution)/shard_map/ppermute | solution.py:193
  29.2 0.8 %collective-permute-done.2.other_ref = s32[8]{0:T(128)S(1)} collective-permute-done((s32[8]{0:T(128)S(1)}, s32[8]{0:T(128)S(1)}, u32[]{:S(2)}, u32[]{:S(2)}) %collective-permute-start.2) | collective-permute-done | bytes 64 | tf_op jit(solution)/shard_map/ppermute | solution.py:193
  30.1 0.0 collective-permute-done.3.came_ref
  30.1 1.7 %coarse.1 = bf16[1,128,512]{2,1,0:T(8,128)(2,1)} custom-call(s32[8]{0:T(128)S(1)} %copy-done.8, s32[8]{0:T(128)S(1)} %collective-permute-done.2.other_ref, bf16[128,512]{1,0:T(8,128)(2,1)S(1)} %get-tuple-element.5.oct_ref, bf16[128,512]{1,0:T(8,128)(2,1)S(1)} %collective-permute-done.3.came_ref), custom_call_target="tpu_custom_call" | custom-call | tf_op jit(solution)/shard_map/coarse/pallas_call | solution.py:234
  (1 shorter events, 0.0 us)
Async XLA Ops:
  0.6 16.4 %copy-start.1 = (bf16[512,1152]{1,0:T(8,128)(2,1)S(1)}, bf16[512,1152]{1,0:T(8,128)(2,1)}, u32[]{:S(2)}) copy-start(bf16[512,1152]{1,0:T(8,128)(2,1)} %constant.16.clone.window_ref) | copy-start | bytes 3538948
  0.6 16.4 %copy-start = (bf16[8,64,512]{2,1,0:T(8,128)(2,1)S(1)}, bf16[8,64,512]{2,1,0:T(8,128)(2,1)}, u32[]{:S(2)}) copy-start(bf16[8,64,512]{2,1,0:T(8,128)(2,1)} %feat_ref.1) | copy-start | bytes 1572868
  0.7 16.4 %copy-start.3 = (s32[8,512]{1,0:T(8,128)S(1)}, s32[8,512]{1,0:T(8,128)}, u32[]{:S(2)}) copy-start(s32[8,512]{1,0:T(8,128)} %occ_ref.1) | copy-start | bytes 49156
  0.7 16.4 %copy-start.5 = (f32[64]{0:T(128)S(1)}, f32[64]{0:T(128)}, u32[]{:S(2)}) copy-start(f32[64]{0:T(128)} %param.15) | copy-start | bytes 772
  0.7 16.4 %copy-start.6 = (f32[64]{0:T(128)S(1)}, f32[64]{0:T(128)}, u32[]{:S(2)}) copy-start(f32[64]{0:T(128)} %param.16) | copy-start | bytes 772
  0.7 16.4 %copy-start.7 = (f32[128]{0:T(128)S(1)}, f32[128]{0:T(128)}, u32[]{:S(2)}) copy-start(f32[128]{0:T(128)} %param.19) | copy-start | bytes 1540
  0.7 16.4 %copy-start.4 = (s32[8,26]{1,0:T(8,128)S(1)}, s32[8,26]{1,0:T(8,128)}, u32[]{:S(2)}) copy-start(s32[8,26]{1,0:T(8,128)} %near_ref.1) | copy-start | bytes 2500
  3.8 7.5 %collective-permute-start = (bf16[8,64,128]{2,1,0:T(8,128)(2,1)S(1)}, bf16[8,64,128]{2,1,0:T(8,128)(2,1)S(1)}, u32[]{:S(2)}, u32[]{:S(2)}) collective-permute-start(bf16[8,64,128]{2,1,0:T(8,128)(2,1)S(1)} %get-tuple-element.9), channel_id=1, source_target_pairs={{0,1},{1,2},{2,3},{3,4},{4,5},{5,6},{6,7},{7,8},{8,9},{9,10},{10,1... | collective-permute-start | bytes 393224 | tf_op jit(solution)/shard_map/ppermute | solution.py:206
  7.2 9.9 %collective-permute-start.1 = (bf16[8,64,128]{2,1,0:T(8,128)(2,1)S(1)}, bf16[8,64,128]{2,1,0:T(8,128)(2,1)S(1)}, u32[]{:S(2)}, u32[]{:S(2)}) collective-permute-start(bf16[8,64,128]{2,1,0:T(8,128)(2,1)S(1)} %get-tuple-element.8), channel_id=1, source_target_pairs={{1,0},{2,1},{3,2},{4,3},{5,4},{6,5},{7,6},{8,7},{9,8},{10,9},{11,1... | collective-permute-start | bytes 393224 | tf_op jit(solution)/shard_map/ppermute | solution.py:207
  17.1 1.0 %copy-start.2 = (bf16[512,512]{1,0:T(8,128)(2,1)S(1)}, bf16[512,512]{1,0:T(8,128)(2,1)}, u32[]{:S(2)}) copy-start(bf16[512,512]{1,0:T(8,128)(2,1)} %constant.17.clone.perm_ref) | copy-start | bytes 1572868
  18.1 10.6 %copy-start.8 = (s32[8]{0:T(128)S(1)}, s32[8]{0:T(128)}, u32[]{:S(2)}) copy-start(s32[8]{0:T(128)} %map_ref.1) | copy-start | bytes 100
  28.7 1.4 %collective-permute-start.3 = (bf16[128,512]{1,0:T(8,128)(2,1)S(1)}, bf16[128,512]{1,0:T(8,128)(2,1)S(1)}, u32[]{:S(2)}, u32[]{:S(2)}) collective-permute-start(bf16[128,512]{1,0:T(8,128)(2,1)S(1)} %get-tuple-element.5.oct_ref), channel_id=1, source_target_pairs={{0,1},{1,0},{2,3},{3,2},{4,5},{5,4},{6,7},{7,6},{8,9},{9,8},{10,11... | collective-permute-start | bytes 393224 | tf_op jit(solution)/shard_map/ppermute | solution.py:193
  28.8 1.3 %collective-permute-start.2 = (s32[8]{0:T(128)S(1)}, s32[8]{0:T(128)S(1)}, u32[]{:S(2)}, u32[]{:S(2)}) collective-permute-start(s32[8]{0:T(128)S(1)} %copy-done.8), channel_id=1, source_target_pairs={{0,1},{1,0},{2,3},{3,2},{4,5},{5,4},{6,7},{7,6},{8,9},{9,8},{10,11... | collective-permute-start | bytes 104 | tf_op jit(solution)/shard_map/ppermute | solution.py:193

commit v2 on v1

v2 whole, which is shorter than its diff:
```python
import jax
import jax.numpy as jnp
import numpy as np
from jax import lax
from jax.experimental import pallas as pl
from jax.experimental.pallas import tpu as pltpu
from jax.sharding import PartitionSpec as P

norm_eps = 1e-06
AXES = ("bricks", "grp")


def window_matrix(shifts, kinds):
    table = np.zeros((4, 2, 64, len(shifts), 2, 64), np.float32)
    for w, (b, c) in enumerate(shifts):
        for y in range(8):
            for z in range(8):
                yy, zz = y + b, z + c
                kind = (1 if not 0 <= yy < 8 else 0) + (2 if not 0 <= zz < 8 else 0)
                for half in range(2):
                    table[kind, half, (yy % 8) * 8 + zz % 8, w, half, y * 8 + z] = 1.0
    return table[kinds].reshape(128 * len(kinds), 128 * len(shifts)).astype(jnp.bfloat16)


def stride_matrix():
    table = np.zeros((512, 512), np.float32)
    for x in range(8):
        for y in range(8):
            for z in range(8):
                tap = 4 * (x % 2) + 2 * (y % 2) + z % 2
                place = 16 * (x // 2) + 4 * (y // 2) + z // 2
                table[64 * x + 8 * y + z, 64 * tap + place] = 1.0
    return table.astype(jnp.bfloat16)


def column(row):
    n = row.shape[1]
    at = lax.broadcasted_iota(jnp.int32, (n, n), 0)
    to = lax.broadcasted_iota(jnp.int32, (n, n), 1)
    return jnp.sum(jnp.where(at == to, row, 0.0), axis=1, keepdims=True)


def offset(dx, dy, dz):
    o = 9 * (dx + 1) + 3 * (dy + 1) + dz + 1
    return o - 1 if o > 13 else o


def dot(a, b):
    return jnp.dot(a, b, preferred_element_type=jnp.float32)


def halos(fetch, masks):
    low_y, low_z = masks
    high_y, high_z = 1 - low_y, 1 - low_z
    halo_y = fetch(1, 0) * low_y + fetch(-1, 0) * high_y
    halo_z = fetch(0, 1) * low_z + fetch(0, -1) * high_z
    near = fetch(1, 1) * low_z + fetch(1, -1) * high_z
    far = fetch(-1, 1) * low_z + fetch(-1, -1) * high_z
    return halo_y, halo_z, near * low_y + far * high_y


def flipped(x):
    n = x.shape[1]
    at = lax.broadcasted_iota(jnp.int32, (n, n), 0)
    to = lax.broadcasted_iota(jnp.int32, (n, n), 1)
    eye = jnp.where(at == to, 1.0, 0.0).astype(jnp.bfloat16)
    dims = (((1,), (1,)), ((), ()))
    return lax.dot_general(eye, x, dims, preferred_element_type=jnp.float32).astype(jnp.bfloat16)


def stack(centre, halo_y, halo_z, corner, side_y, side_z, side_yz):
    tiles = centre.shape[0] // 64
    pair_y = dot(jnp.concatenate([centre, halo_y], axis=1), side_y).astype(jnp.bfloat16)
    pair_z = dot(jnp.concatenate([centre, halo_z], axis=1), side_z).astype(jnp.bfloat16)
    four = jnp.concatenate([centre, halo_y, halo_z, corner], axis=1)
    quad = dot(four, side_yz).astype(jnp.bfloat16)
    order = [
        (quad, 0), (pair_y, 0), (quad, 1), (pair_z, 0), (centre, 0),
        (pair_z, 1), (quad, 2), (pair_y, 1), (quad, 3),
    ]
    return jnp.concatenate(
        [
            jnp.concatenate(
                [m[64 * p : 64 * p + 64, 128 * w : 128 * w + 128] for m, w in order], axis=0
            )
            for p in range(tiles)
        ],
        axis=1,
    )


def place(keys, octants, coarse, count):
    k = lax.broadcasted_iota(jnp.int32, (64, 512), 0)
    lane = lax.broadcasted_iota(jnp.int32, (64, 512), 1)
    rest = lane - (64 * (k >> 4) + 8 * ((k >> 2) & 3) + (k & 3))
    o = keys & 7
    starts = 256 * (o >> 2) + 32 * ((o >> 1) & 1) + 4 * (o & 1)
    starts = jnp.where((keys >> 3) == coarse, starts, -1024)
    starts = jnp.concatenate([starts] * 4, axis=1)
    blocks = [
        jnp.where(rest == starts[j : j + 1], 1.0, 0.0).astype(jnp.bfloat16) for j in range(count)
    ]
    return dot(octants, jnp.concatenate(blocks, axis=0))


def kernel(
    near_ref, occ_ref, map_ref, gain_ref, shift_ref, bias_ref,
    feat_hbm, weight_hbm, stride_hbm, side_y_hbm, side_z_hbm, side_yz_hbm, perm_hbm,
    fine_hbm, coarse_ref,
    feat, weight, stride, side_y, side_z, side_yz, perm,
    act, lower, upper, conv, fine, weight_t, keys, keys_in, octs, octs_in,
    local_sem, send_sem, recv_sem,
):
    count = feat.shape[0]
    groups = lax.axis_size("grp")
    peers = groups * lax.axis_size("bricks")
    device = lax.axis_index("bricks") * groups + lax.axis_index("grp")
    has_left = device > 0
    has_right = device < peers - 1

    def coords(other):
        return {"bricks": other // groups, "grp": other % groups}

    loads = [
        pltpu.make_async_copy(src, dst, local_sem.at[n])
        for n, (src, dst) in enumerate(
            [
                (feat_hbm, feat), (weight_hbm, weight), (side_y_hbm, side_y),
                (side_z_hbm, side_z), (side_yz_hbm, side_yz), (perm_hbm, perm),
                (stride_hbm, stride),
            ]
        )
    ]
    for load in loads:
        load.start()
    barrier = pltpu.get_barrier_semaphore()

    @pl.when(has_left)
    def _():
        pl.semaphore_signal(
            barrier, inc=1, device_id=coords(device - 1), device_id_type=pl.DeviceIdType.MESH
        )

    @pl.when(has_right)
    def _():
        pl.semaphore_signal(
            barrier, inc=1, device_id=coords(device + 1), device_id_type=pl.DeviceIdType.MESH
        )

    gain = column(gain_ref[...])
    shift = column(shift_ref[...])
    bias = column(bias_ref[...])
    keys[...] = jnp.broadcast_to(
        column(map_ref[...].astype(jnp.float32)).astype(jnp.int32), keys.shape
    )
    act[count] = jnp.zeros((64, 512), jnp.bfloat16)
    lower[count] = jnp.zeros((64, 128), jnp.bfloat16)
    upper[count] = jnp.zeros((64, 128), jnp.bfloat16)

    @pl.when(jnp.logical_not(has_left))
    def _():
        lower[0:count] = jnp.zeros((count, 64, 128), jnp.bfloat16)

    @pl.when(jnp.logical_not(has_right))
    def _():
        upper[0:count] = jnp.zeros((count, 64, 128), jnp.bfloat16)

    loads[0].wait()

    def activate_one(i, carry):
        values = feat[i].astype(jnp.float32)
        scale = lax.rsqrt(jnp.mean(values * values, axis=0, keepdims=True) + norm_eps)
        normed = values * scale * gain
        mask = occ_ref[pl.ds(i, 1), :].astype(jnp.float32)
        act[i] = (normed / (1.0 + jnp.exp(-normed)) * mask).astype(jnp.bfloat16)
        return carry

    lax.fori_loop(0, count, activate_one, 0)

    def remote(n, src, dst, other):
        return pltpu.make_async_remote_copy(
            src_ref=src, dst_ref=dst, send_sem=send_sem.at[n], recv_sem=recv_sem.at[n],
            device_id=coords(other), device_id_type=pl.DeviceIdType.MESH,
        )

    bricks = pl.ds(0, count)
    rise = remote(0, act.at[bricks, :, pl.ds(384, 128)], lower.at[bricks], device + 1)
    fall = remote(1, act.at[bricks, :, pl.ds(0, 128)], upper.at[bricks], device - 1)
    mate = device + 1 - 2 * (device % 2)
    swap_keys = remote(2, keys, keys_in, mate)
    swap_octs = remote(3, octs, octs_in, mate)

    pl.semaphore_wait(barrier, has_left.astype(jnp.int32) + has_right.astype(jnp.int32))

    @pl.when(has_right)
    def _():
        rise.start()

    @pl.when(has_left)
    def _():
        fall.start()

    swap_keys.start()

    for load in loads[1:]:
        load.wait()
    for a in range(3):
        weight_t[64 * a : 64 * a + 64] = flipped(weight[576 * a : 576 * a + 576])

    lane = lax.broadcasted_iota(jnp.int32, (64, 512), 1)
    low_y = jnp.where(lane % 64 < 32, 1.0, 0.0).astype(jnp.bfloat16)
    low_z = jnp.where(lane % 8 < 4, 1.0, 0.0).astype(jnp.bfloat16)
    half = lax.broadcasted_iota(jnp.int32, (64, 128), 1) < 64
    first = jnp.where(half, 1.0, 0.0).astype(jnp.bfloat16)
    second = 1 - first

    def row(i, dx, dy, dz):
        target = near_ref[i, offset(dx, dy, dz)]
        local = jnp.clip(target - (device + dx) * count, 0, count - 1)
        return jnp.where(target < 0, count, local)

    def middle(i, carry):
        def own(dy, dz):
            return act[row(i, 0, dy, dz)]

        wide = (act[i],) + halos(own, (low_y, low_z))
        tall = [
            jnp.concatenate([m[:, 128 * p : 128 * p + 128] for p in range(4)], axis=0)
            for m in wide
        ]
        stacked = stack(*tall, side_y[...], side_z[...], side_yz[...])
        product = dot(weight_t[...], stacked)

        def part(dx, p):
            if not 0 <= p < 4:
                return jnp.zeros((64, 128), jnp.float32)
            return product[64 * (dx + 1) : 64 * (dx + 2), 128 * p : 128 * p + 128]

        pieces = []
        for p in range(4):
            below = pltpu.roll(jnp.where(half, part(-1, p), part(-1, p - 1)), 64, 1)
            above = pltpu.roll(jnp.where(half, part(1, p + 1), part(1, p)), 64, 1)
            pieces.append(part(0, p) + below + above)
        conv[i] = jnp.concatenate(pieces, axis=1)
        return carry

    lax.fori_loop(0, count, middle, 0, unroll=2)

    @pl.when(has_left)
    def _():
        rise.wait_recv()
        fall.wait_send()

    @pl.when(has_right)
    def _():
        fall.wait_recv()
        rise.wait_send()

    step = 4

    def edges(g, carry):
        tall = [[], [], [], []]
        for n in range(step):
            i = g * step + n

            def outer(dy, dz):
                return upper[row(i, 1, dy, dz)] * first + lower[row(i, -1, dy, dz)] * second

            edge = (outer(0, 0),) + halos(outer, (low_y[:, :128], low_z[:, :128]))
            for into, piece in zip(tall, edge):
                into.append(piece)
        tall = [jnp.concatenate(m, axis=0) for m in tall]
        stacked = stack(*tall, side_y[...], side_z[...], side_yz[...])
        outside = jnp.concatenate([weight_t[0:64], weight_t[128:192]], axis=0)
        product = dot(outside, stacked)
        for n in range(step):
            i = g * step + n
            mine = product[:, 128 * n : 128 * n + 128]
            turned = pltpu.roll(jnp.where(half, mine[64:], mine[:64]), 64, 1)
            mask = occ_ref[pl.ds(i, 1), :].astype(jnp.float32)
            summed = feat[i].astype(jnp.float32) + conv[i] + shift
            ends = jnp.concatenate(
                [
                    jnp.where(half, turned, 0.0),
                    jnp.zeros((64, 256), jnp.float32),
                    jnp.where(half, 0.0, turned),
                ],
                axis=1,
            )
            fine[i] = (mask * (summed + ends)).astype(jnp.bfloat16)
        return carry

    lax.fori_loop(0, count // step, edges, 0)
    store = pltpu.make_async_copy(fine, fine_hbm, local_sem.at[len(loads)])
    store.start()

    ordered = dot(fine[...].reshape(count * 64, 512), perm[...])
    columns = []
    for j in range(0, count, 2):
        taps = []
        for s in range(4):
            one = ordered[64 * j : 64 * j + 64, 128 * s : 128 * s + 128]
            two = ordered[64 * j + 64 : 64 * j + 128, 128 * s : 128 * s + 128]
            taps.append(jnp.where(half, one, pltpu.roll(two, 64, 1)))
            taps.append(jnp.where(half, pltpu.roll(one, 64, 1), two))
        columns.append(jnp.concatenate(taps, axis=0).astype(jnp.bfloat16))
    octants = dot(flipped(stride[...]), jnp.concatenate(columns, axis=1)) + bias
    octs[...] = octants.astype(jnp.bfloat16)
    swap_octs.start()
    total = place(keys[...], octs[...], device, count)
    swap_keys.wait()
    swap_octs.wait()
    total = total + place(keys_in[...], octs_in[...], device, count)
    coarse_ref[0] = total.astype(jnp.bfloat16)
    store.wait()


def shards(
    features, occupancy, neighbours, coarse_map, norm_gain, time_shift, conv_weight,
    stride_weight, coarse_bias,
):
    count = features.shape[0]
    bf16 = jnp.bfloat16
    vmem = pl.BlockSpec(memory_space=pltpu.VMEM)
    smem = pl.BlockSpec(memory_space=pltpu.SMEM)
    hbm = pl.BlockSpec(memory_space=pl.ANY)
    side_y = window_matrix([(-1, 0), (1, 0)], [0, 1])
    side_z = window_matrix([(0, -1), (0, 1)], [0, 2])
    side_yz = window_matrix([(-1, -1), (-1, 1), (1, -1), (1, 1)], [0, 1, 2, 3])
    return pl.pallas_call(
        kernel,
        out_shape=(
            jax.ShapeDtypeStruct(features.shape, bf16),
            jax.ShapeDtypeStruct((1, 128, 512), bf16),
        ),
        in_specs=[smem] + [vmem] * 5 + [hbm] * 7,
        out_specs=(hbm, vmem),
        scratch_shapes=[
            pltpu.VMEM((count, 64, 512), bf16),
            pltpu.VMEM((1728, 64), bf16),
            pltpu.VMEM((512, 128), bf16),
            pltpu.VMEM((256, 256), bf16),
            pltpu.VMEM((256, 256), bf16),
            pltpu.VMEM((512, 512), bf16),
            pltpu.VMEM((512, 512), bf16),
            pltpu.VMEM((count + 1, 64, 512), bf16),
            pltpu.VMEM((count + 1, 64, 128), bf16),
            pltpu.VMEM((count + 1, 64, 128), bf16),
            pltpu.VMEM((count, 64, 512), jnp.float32),
            pltpu.VMEM((count, 64, 512), bf16),
            pltpu.VMEM((192, 576), bf16),
            pltpu.VMEM((count, 128), jnp.int32),
            pltpu.VMEM((count, 128), jnp.int32),
            pltpu.VMEM((128, 64 * count), bf16),
            pltpu.VMEM((128, 64 * count), bf16),
            pltpu.SemaphoreType.DMA((8,)),
            pltpu.SemaphoreType.DMA((4,)),
            pltpu.SemaphoreType.DMA((4,)),
        ],
        compiler_params=pltpu.CompilerParams(
            collective_id=0, has_side_effects=True, vmem_limit_bytes=48 * 1024 * 1024
        ),
        name="bricks",
    )(
        neighbours, occupancy, coarse_map[None], norm_gain[None], time_shift[None],
        coarse_bias[None], features, conv_weight.reshape(1728, 64),
        stride_weight.reshape(512, 128), side_y, side_z, side_yz, stride_matrix(),
    )


def solution(mesh):
    wide = P(AXES, None, None)
    return jax.shard_map(
        shards,
        mesh=mesh,
        in_specs=(wide, P(AXES, None), P(AXES, None), P(AXES), P(), P(), P(), P(), P()),
        out_specs=(wide, wide),
        check_vma=False,
    )
```

time: 32.1 us -> 25.8 us (0.80)
  the two profiles are of different devices: /device:TPU:27 before, /device:TPU:5 now
where the time goes in v2:
time: 25.8 us; the launch traced here: 25.3 us
  Pallas kernels  15 us (58%)
  local copies, waits for them, and re-layouts  9.69 us (38%)
  between operations  0.69 us (3%)
    pallas_call x1, Pallas kernels, shards(): pl.pallas_call(kernel, out_shape=(jax.ShapeDtypeStruct(features.shape, bf...  15 us
    unnamed x28, local copies, waits for them, and re-layouts  9.69 us

profile of v2, /device:TPU:5, one launch (start us, length us, event | category | flops | bytes accessed | tf_op | source)
XLA Modules:
  0.0 25.3 jit_solution(3815897833701793317)
XLA Ops:
  0.6 0.0 copy-start.8
  0.6 0.0 copy-start.12
  0.7 0.0 copy-start.9
  0.7 0.0 copy-start.10
  0.7 0.0 copy-start.11
  0.7 0.6 %copy-done.8 = s32[8,26]{1,0:T(8,128)S(1)} copy-done((s32[8,26]{1,0:T(8,128)S(1)}, s32[8,26]{1,0:T(8,128)}, u32[]{:S(2)}) %copy-start.8) | copy-done | bytes 856
  1.3 0.0 copy-done.12
  1.3 0.0 copy-done.9
  1.3 0.0 copy-done.10
  1.3 0.0 copy-done.11
  1.4 0.0 copy-start
  1.4 1.0 %copy-done = bf16[8,64,512]{2,1,0:T(8,128)(2,1)S(1)} copy-done((bf16[8,64,512]{2,1,0:T(8,128)(2,1)S(1)}, bf16[8,64,512]{2,1,0:T(8,128)(2,1)}, u32[]{:S(2)}) %copy-start) | copy-done | bytes 524312
  2.4 0.0 copy-start.1
  2.4 1.0 %copy-done.1 = bf16[512,512]{1,0:T(8,128)(2,1)S(1)} copy-done((bf16[512,512]{1,0:T(8,128)(2,1)S(1)}, bf16[512,512]{1,0:T(8,128)(2,1)}, u32[]{:S(2)}) %copy-start.1) | copy-done | bytes 524312
  3.4 0.0 copy-start.2
  3.4 1.0 %copy-done.2 = bf16[512,512]{1,0:T(8,128)(2,1)S(1)} copy-done((bf16[512,512]{1,0:T(8,128)(2,1)S(1)}, bf16[512,512]{1,0:T(8,128)(2,1)}, u32[]{:S(2)}) %copy-start.2) | copy-done | bytes 524312
  4.5 0.0 copy-start.3
  4.5 1.0 %copy-done.3 = bf16[27,64,64]{2,1,0:T(8,128)(2,1)S(1)} copy-done((bf16[27,64,64]{2,1,0:T(8,128)(2,1)S(1)}, bf16[27,64,64]{2,1,0:T(8,128)(2,1)}, u32[]{:S(2)}) %copy-start.3) | copy-done | bytes 221208
  5.5 0.0 copy-start.4
  5.5 0.9 %copy-done.4 = bf16[8,64,128]{2,1,0:T(8,128)(2,1)S(1)} copy-done((bf16[8,64,128]{2,1,0:T(8,128)(2,1)S(1)}, bf16[8,64,128]{2,1,0:T(8,128)(2,1)}, u32[]{:S(2)}) %copy-start.4) | copy-done | bytes 131096
  6.4 0.0 copy-start.5
  6.4 0.9 %copy-done.5 = bf16[256,256]{1,0:T(8,128)(2,1)S(1)} copy-done((bf16[256,256]{1,0:T(8,128)(2,1)S(1)}, bf16[256,256]{1,0:T(8,128)(2,1)}, u32[]{:S(2)}) %copy-start.5) | copy-done | bytes 131096
  7.3 0.0 copy-start.6
  7.3 0.9 %copy-done.6 = bf16[256,256]{1,0:T(8,128)(2,1)S(1)} copy-done((bf16[256,256]{1,0:T(8,128)(2,1)S(1)}, bf16[256,256]{1,0:T(8,128)(2,1)}, u32[]{:S(2)}) %copy-start.6) | copy-done | bytes 131096
  8.2 0.0 copy-start.7
  8.2 0.7 %copy-done.7 = s32[8,512]{1,0:T(8,128)S(1)} copy-done((s32[8,512]{1,0:T(8,128)S(1)}, s32[8,512]{1,0:T(8,128)}, u32[]{:S(2)}) %copy-start.7) | copy-done | bytes 16408
  8.9 15.0 %bricks.1 = (bf16[8,64,512]{2,1,0:T(8,128)(2,1)S(1)}, bf16[1,128,512]{2,1,0:T(8,128)(2,1)S(1)}) custom-call(s32[8,26]{1,0:T(8,128)S(1)} %copy-done.8, s32[8,512]{1,0:T(8,128)S(1)} %copy-done.7, s32[1,8]{1,0:T(1,128)S(1)} %bitcast.8, f32[1,64]{1,0:T(1,128)S(1)} %bitcast.9, f32[1,64]{1,0:T(1,128)S(1)} %bitcast.10, f32[1,128]{1,0:T(1,128)S(1)} %bitcast.11, ...), custom_call_target="tpu_custom_call" | custom-call | tf_op jit(solution)/shard_map/bricks/pallas_call | solution.py:330
  23.9 0.8 %copy.17 = bf16[8,64,512]{2,1,0:T(8,128)(2,1)} copy(bf16[8,64,512]{2,1,0:T(8,128)(2,1)S(1)} %get-tuple-element.4) | data formatting | bytes 1048576
  24.7 0.7 %copy.18 = bf16[1,128,512]{2,1,0:T(8,128)(2,1)} copy(bf16[1,128,512]{2,1,0:T(8,128)(2,1)S(1)} %get-tuple-element.5) | data formatting | bytes 262144
Async XLA Ops:
  0.6 0.7 %copy-start.8 = (s32[8,26]{1,0:T(8,128)S(1)}, s32[8,26]{1,0:T(8,128)}, u32[]{:S(2)}) copy-start(s32[8,26]{1,0:T(8,128)} %near_ref.1) | copy-start | bytes 2500
  0.6 0.7 %copy-start.12 = (f32[128]{0:T(128)S(1)}, f32[128]{0:T(128)}, u32[]{:S(2)}) copy-start(f32[128]{0:T(128)} %param.21) | copy-start | bytes 1540
  0.7 0.7 %copy-start.9 = (s32[8]{0:T(128)S(1)}, s32[8]{0:T(128)}, u32[]{:S(2)}) copy-start(s32[8]{0:T(128)} %param.16) | copy-start | bytes 100
  0.7 0.7 %copy-start.10 = (f32[64]{0:T(128)S(1)}, f32[64]{0:T(128)}, u32[]{:S(2)}) copy-start(f32[64]{0:T(128)} %param.17) | copy-start | bytes 772
  0.7 0.7 %copy-start.11 = (f32[64]{0:T(128)S(1)}, f32[64]{0:T(128)}, u32[]{:S(2)}) copy-start(f32[64]{0:T(128)} %param.18) | copy-start | bytes 772
  1.4 1.0 %copy-start = (bf16[8,64,512]{2,1,0:T(8,128)(2,1)S(1)}, bf16[8,64,512]{2,1,0:T(8,128)(2,1)}, u32[]{:S(2)}) copy-start(bf16[8,64,512]{2,1,0:T(8,128)(2,1)} %feat_hbm.1) | copy-start | bytes 1572868
  2.4 1.0 %copy-start.1 = (bf16[512,512]{1,0:T(8,128)(2,1)S(1)}, bf16[512,512]{1,0:T(8,128)(2,1)}, u32[]{:S(2)}) copy-start(bf16[512,512]{1,0:T(8,128)(2,1)} %constant.11.clone.perm_hbm) | copy-start | bytes 1572868
  3.4 1.0 %copy-start.2 = (bf16[512,512]{1,0:T(8,128)(2,1)S(1)}, bf16[512,512]{1,0:T(8,128)(2,1)}, u32[]{:S(2)}) copy-start(bf16[512,512]{1,0:T(8,128)(2,1)} %constant.10.clone.side_yz_hbm) | copy-start | bytes 1572868
  4.5 1.0 %copy-start.3 = (bf16[27,64,64]{2,1,0:T(8,128)(2,1)S(1)}, bf16[27,64,64]{2,1,0:T(8,128)(2,1)}, u32[]{:S(2)}) copy-start(bf16[27,64,64]{2,1,0:T(8,128)(2,1)} %param.19) | copy-start | bytes 663556
  5.5 0.9 %copy-start.4 = (bf16[8,64,128]{2,1,0:T(8,128)(2,1)S(1)}, bf16[8,64,128]{2,1,0:T(8,128)(2,1)}, u32[]{:S(2)}) copy-start(bf16[8,64,128]{2,1,0:T(8,128)(2,1)} %param.20) | copy-start | bytes 393220
  6.4 0.9 %copy-start.5 = (bf16[256,256]{1,0:T(8,128)(2,1)S(1)}, bf16[256,256]{1,0:T(8,128)(2,1)}, u32[]{:S(2)}) copy-start(bf16[256,256]{1,0:T(8,128)(2,1)} %constant.9.clone.side_z_hbm) | copy-start | bytes 393220
  7.3 0.9 %copy-start.6 = (bf16[256,256]{1,0:T(8,128)(2,1)S(1)}, bf16[256,256]{1,0:T(8,128)(2,1)}, u32[]{:S(2)}) copy-start(bf16[256,256]{1,0:T(8,128)(2,1)} %constant.8.clone.side_y_hbm) | copy-start | bytes 393220
  8.2 0.7 %copy-start.7 = (s32[8,512]{1,0:T(8,128)S(1)}, s32[8,512]{1,0:T(8,128)}, u32[]{:S(2)}) copy-start(s32[8,512]{1,0:T(8,128)} %occ_ref.1) | copy-start | bytes 49156

commit v3 on v2

--- a/solution.py
+++ b/solution.py
@@ -89,7 +89,7 @@
     )
 
 
-def place(keys, octants, coarse, count):
+def place(keys, near, far, coarse, count):
     k = lax.broadcasted_iota(jnp.int32, (64, 512), 0)
     lane = lax.broadcasted_iota(jnp.int32, (64, 512), 1)
     rest = lane - (64 * (k >> 4) + 8 * ((k >> 2) & 3) + (k & 3))
@@ -100,15 +100,17 @@
     blocks = [
         jnp.where(rest == starts[j : j + 1], 1.0, 0.0).astype(jnp.bfloat16) for j in range(count)
     ]
+    octants = jnp.concatenate([near, far], axis=1)
     return dot(octants, jnp.concatenate(blocks, axis=0))
 
 
 def kernel(
-    near_ref, occ_ref, map_ref, gain_ref, shift_ref, bias_ref,
-    feat_hbm, weight_hbm, stride_hbm, side_y_hbm, side_z_hbm, side_yz_hbm, perm_hbm,
-    fine_hbm, coarse_ref,
-    feat, weight, stride, side_y, side_z, side_yz, perm,
-    act, lower, upper, conv, fine, weight_t, keys, keys_in, octs, octs_in,
+    occ_hbm, gain_hbm, feat_hbm, map_hbm, near_hbm, weight_hbm, side_y_hbm, side_z_hbm,
+    side_yz_hbm, perm_hbm, stride_hbm, shift_hbm, bias_hbm,
+    fine_hbm, coarse_hbm,
+    occ_ref, gain_ref, feat, map_ref, near_ref, weight, side_y, side_z,
+    side_yz, perm, stride, shift_ref, bias_ref,
+    act, lower, upper, conv, fine, coarse, weight_t, keys, keys_in, octs, octs_in,
     local_sem, send_sem, recv_sem,
 ):
     count = feat.shape[0]
@@ -125,9 +127,10 @@
         pltpu.make_async_copy(src, dst, local_sem.at[n])
         for n, (src, dst) in enumerate(
             [
-                (feat_hbm, feat), (weight_hbm, weight), (side_y_hbm, side_y),
+                (occ_hbm, occ_ref), (gain_hbm, gain_ref), (feat_hbm, feat), (map_hbm, map_ref),
+                (near_hbm, near_ref), (weight_hbm, weight), (side_y_hbm, side_y),
                 (side_z_hbm, side_z), (side_yz_hbm, side_yz), (perm_hbm, perm),
-                (stride_hbm, stride),
+                (stride_hbm, stride), (shift_hbm, shift_ref), (bias_hbm, bias_ref),
             ]
         )
     ]
@@ -147,12 +150,6 @@
             barrier, inc=1, device_id=coords(device + 1), device_id_type=pl.DeviceIdType.MESH
         )
 
-    gain = column(gain_ref[...])
-    shift = column(shift_ref[...])
-    bias = column(bias_ref[...])
-    keys[...] = jnp.broadcast_to(
-        column(map_ref[...].astype(jnp.float32)).astype(jnp.int32), keys.shape
-    )
     act[count] = jnp.zeros((64, 512), jnp.bfloat16)
     lower[count] = jnp.zeros((64, 128), jnp.bfloat16)
     upper[count] = jnp.zeros((64, 128), jnp.bfloat16)
@@ -165,7 +162,9 @@
     def _():
         upper[0:count] = jnp.zeros((count, 64, 128), jnp.bfloat16)
 
-    loads[0].wait()
+    for load in loads[:3]:
+        load.wait()
+    gain = column(gain_ref[...])
 
     def activate_one(i, carry):
         values = feat[i].astype(jnp.float32)
@@ -175,7 +174,11 @@
         act[i] = (normed / (1.0 + jnp.exp(-normed)) * mask).astype(jnp.bfloat16)
         return carry
 
-    lax.fori_loop(0, count, activate_one, 0)
+    lax.fori_loop(0, count, activate_one, 0, unroll=2)
+    loads[3].wait()
+    keys[...] = jnp.broadcast_to(
+        column(map_ref[...].astype(jnp.float32)).astype(jnp.int32), keys.shape
+    )
 
     def remote(n, src, dst, other):
         return pltpu.make_async_remote_copy(
@@ -188,7 +191,6 @@
     fall = remote(1, act.at[bricks, :, pl.ds(0, 128)], upper.at[bricks], device - 1)
     mate = device + 1 - 2 * (device % 2)
     swap_keys = remote(2, keys, keys_in, mate)
-    swap_octs = remote(3, octs, octs_in, mate)
 
     pl.semaphore_wait(barrier, has_left.astype(jnp.int32) + has_right.astype(jnp.int32))
 
@@ -202,8 +204,11 @@
 
     swap_keys.start()
 
-    for load in loads[1:]:
+    for load in loads[4:]:
         load.wait()
+    shift = column(shift_ref[...])
+    bias = column(bias_ref[...])
+    stride_t = flipped(stride[...])
     for a in range(3):
         weight_t[64 * a : 64 * a + 64] = flipped(weight[576 * a : 576 * a + 576])
 
@@ -256,9 +261,12 @@
         fall.wait_recv()
         rise.wait_send()
 
-    step = 4
-
-    def edges(g, carry):
+    step = count // 2
+    outside = jnp.concatenate([weight_t[0:64], weight_t[128:192]], axis=0)
+    sent = []
+    stores = []
+    for g in range(2):
+        group = pl.ds(g * step, step)
         tall = [[], [], [], []]
         for n in range(step):
             i = g * step + n
@@ -271,7 +279,6 @@
                 into.append(piece)
         tall = [jnp.concatenate(m, axis=0) for m in tall]
         stacked = stack(*tall, side_y[...], side_z[...], side_yz[...])
-        outside = jnp.concatenate([weight_t[0:64], weight_t[128:192]], axis=0)
         product = dot(outside, stacked)
         for n in range(step):
             i = g * step + n
@@ -288,31 +295,38 @@
                 axis=1,
             )
             fine[i] = (mask * (summed + ends)).astype(jnp.bfloat16)
-        return carry
-
-    lax.fori_loop(0, count // step, edges, 0)
-    store = pltpu.make_async_copy(fine, fine_hbm, local_sem.at[len(loads)])
+        store = pltpu.make_async_copy(
+            fine.at[group], fine_hbm.at[group], local_sem.at[len(loads) + g]
+        )
+        store.start()
+        stores.append(store)
+
+        ordered = dot(fine[group].reshape(step * 64, 512), perm[...])
+        columns = []
+        for j in range(0, step, 2):
+            taps = []
+            for s in range(4):
+                one = ordered[64 * j : 64 * j + 64, 128 * s : 128 * s + 128]
+                two = ordered[64 * j + 64 : 64 * j + 128, 128 * s : 128 * s + 128]
+                taps.append(jnp.where(half, one, pltpu.roll(two, 64, 1)))
+                taps.append(jnp.where(half, pltpu.roll(one, 64, 1), two))
+            columns.append(jnp.concatenate(taps, axis=0).astype(jnp.bfloat16))
+        octants = dot(stride_t, jnp.concatenate(columns, axis=1)) + bias
+        octs[g] = octants.astype(jnp.bfloat16)
+        swap = remote(3 + g, octs.at[g], octs_in.at[g], mate)
+        swap.start()
+        sent.append(swap)
+
+    total = place(keys[...], octs[0], octs[1], device, count)
+    swap_keys.wait()
+    for swap in sent:
+        swap.wait()
+    total = total + place(keys_in[...], octs_in[0], octs_in[1], device, count)
+    coarse[0] = total.astype(jnp.bfloat16)
+    store = pltpu.make_async_copy(coarse, coarse_hbm, local_sem.at[len(loads) + 2])
     store.start()
-
-    ordered = dot(fine[...].reshape(count * 64, 512), perm[...])
-    columns = []
-    for j in range(0, count, 2):
-        taps = []
-        for s in range(4):
-            one = ordered[64 * j : 64 * j + 64, 128 * s : 128 * s + 128]
-            two = ordered[64 * j + 64 : 64 * j + 128, 128 * s : 128 * s + 128]
-            taps.append(jnp.where(half, one, pltpu.roll(two, 64, 1)))
-            taps.append(jnp.where(half, pltpu.roll(one, 64, 1), two))
-        columns.append(jnp.concatenate(taps, axis=0).astype(jnp.bfloat16))
-    octants = dot(flipped(stride[...]), jnp.concatenate(columns, axis=1)) + bias
-    octs[...] = octants.astype(jnp.bfloat16)
-    swap_octs.start()
-    total = place(keys[...], octs[...], device, count)
-    swap_keys.wait()
-    swap_octs.wait()
-    total = total + place(keys_in[...], octs_in[...], device, count)
-    coarse_ref[0] = total.astype(jnp.bfloat16)
-    store.wait()
+    for store in stores + [store]:
+        store.wait()
 
 
 def shards(
@@ -321,8 +335,6 @@
 ):
     count = features.shape[0]
     bf16 = jnp.bfloat16
-    vmem = pl.BlockSpec(memory_space=pltpu.VMEM)
-    smem = pl.BlockSpec(memory_space=pltpu.SMEM)
     hbm = pl.BlockSpec(memory_space=pl.ANY)
     side_y = window_matrix([(-1, 0), (1, 0)], [0, 1])
     side_z = window_matrix([(0, -1), (0, 1)], [0, 2])
@@ -333,38 +345,45 @@
             jax.ShapeDtypeStruct(features.shape, bf16),
             jax.ShapeDtypeStruct((1, 128, 512), bf16),
         ),
-        in_specs=[smem] + [vmem] * 5 + [hbm] * 7,
-        out_specs=(hbm, vmem),
+        in_specs=[hbm] * 13,
+        out_specs=(hbm, hbm),
         scratch_shapes=[
+            pltpu.VMEM((count, 512), jnp.int32),
+            pltpu.VMEM((1, 64), jnp.float32),
             pltpu.VMEM((count, 64, 512), bf16),
+            pltpu.VMEM((1, count), jnp.int32),
+            pltpu.SMEM((count, 26), jnp.int32),
             pltpu.VMEM((1728, 64), bf16),
-            pltpu.VMEM((512, 128), bf16),
             pltpu.VMEM((256, 256), bf16),
             pltpu.VMEM((256, 256), bf16),
             pltpu.VMEM((512, 512), bf16),
             pltpu.VMEM((512, 512), bf16),
+            pltpu.VMEM((512, 128), bf16),
+            pltpu.VMEM((1, 64), jnp.float32),
+            pltpu.VMEM((1, 128), jnp.float32),
             pltpu.VMEM((count + 1, 64, 512), bf16),
             pltpu.VMEM((count + 1, 64, 128), bf16),
             pltpu.VMEM((count + 1, 64, 128), bf16),
             pltpu.VMEM((count, 64, 512), jnp.float32),
             pltpu.VMEM((count, 64, 512), bf16),
+            pltpu.VMEM((1, 128, 512), bf16),
             pltpu.VMEM((192, 576), bf16),
             pltpu.VMEM((count, 128), jnp.int32),
             pltpu.VMEM((count, 128), jnp.int32),
-            pltpu.VMEM((128, 64 * count), bf16),
-            pltpu.VMEM((128, 64 * count), bf16),
-            pltpu.SemaphoreType.DMA((8,)),
-            pltpu.SemaphoreType.DMA((4,)),
-            pltpu.SemaphoreType.DMA((4,)),
+            pltpu.VMEM((2, 128, 32 * count), bf16),
+            pltpu.VMEM((2, 128, 32 * count), bf16),
+            pltpu.SemaphoreType.DMA((16,)),
+            pltpu.SemaphoreType.DMA((5,)),
+            pltpu.SemaphoreType.DMA((5,)),
         ],
         compiler_params=pltpu.CompilerParams(
-            collective_id=0, has_side_effects=True, vmem_limit_bytes=48 * 1024 * 1024
+            collective_id=0, has_side_effects=True, vmem_limit_bytes=63 * 1024 * 1024
         ),
         name="bricks",
     )(
-        neighbours, occupancy, coarse_map[None], norm_gain[None], time_shift[None],
-        coarse_bias[None], features, conv_weight.reshape(1728, 64),
-        stride_weight.reshape(512, 128), side_y, side_z, side_yz, stride_matrix(),
+        occupancy, norm_gain[None], features, coarse_map[None], neighbours,
+        conv_weight.reshape(1728, 64), side_y, side_z, side_yz, stride_matrix(),
+        stride_weight.reshape(512, 128), time_shift[None], coarse_bias[None],
     )
 
 

time: 25.8 us -> 18.1 us (0.70)
  local copies, waits for them, and re-layouts: 9.69 us -> 2.56 us
  Pallas kernels: 15 us -> 14.6 us
    unnamed x28 -> x4, local copies, waits for them, and re-layouts: 9.69 us -> 2.56 us
    pallas_call x1, Pallas kernels: 15 us -> 14.6 us  [shards(): pl.pallas_call(kernel, out_shape=(jax.ShapeDtypeStruct(features.shape, bf...]
where the time goes in v3:
time: 18.1 us; the launch traced here: 17.8 us
  Pallas kernels  14.6 us (81%)
  local copies, waits for them, and re-layouts  2.56 us (14%)
  between operations  0.65 us (4%)
    pallas_call x1, Pallas kernels, shards(): pl.pallas_call(kernel, out_shape=(jax.ShapeDtypeStruct(features.shape, bf...  14.6 us
    unnamed x4, local copies, waits for them, and re-layouts  2.56 us

profile of v3, /device:TPU:5, one launch (start us, length us, event | category | flops | bytes accessed | tf_op | source)
XLA Modules:
  0.0 17.8 jit_solution(14972293341384738227)
XLA Ops:
  0.6 14.6 %bricks.1 = (bf16[8,64,512]{2,1,0:T(8,128)(2,1)}, bf16[1,128,512]{2,1,0:T(8,128)(2,1)}) custom-call(s32[8,512]{1,0:T(8,128)} %occ_hbm.1, f32[1,64]{1,0:T(1,128)} %bitcast.8, bf16[8,64,512]{2,1,0:T(8,128)(2,1)} %feat_hbm.1, s32[1,8]{1,0:T(1,128)} %bitcast.9, s32[8,26]{1,0:T(8,128)} %near_hbm.1, bf16[1728,64]{1,0:T(8,128)(2,1)} %bitcast.6, ...), custom_call_target="tpu_custom_call" | custom-call | tf_op jit(solution)/shard_map/bricks/pallas_call | solution.py:342
  15.2 0.0 copy-start
  15.3 1.9 %copy.17 = bf16[8,64,512]{2,1,0:T(8,128)(2,1)} copy(bf16[8,64,512]{2,1,0:T(8,128)(2,1)} %get-tuple-element.4) | data formatting | bytes 1048576
  17.2 0.0 copy-done
  17.2 0.7 %copy.18 = bf16[1,128,512]{2,1,0:T(8,128)(2,1)} copy(bf16[1,128,512]{2,1,0:T(8,128)(2,1)S(1)} %copy-done) | data formatting | bytes 262144
Async XLA Ops:
  15.2 1.9 %copy-start = (bf16[1,128,512]{2,1,0:T(8,128)(2,1)S(1)}, bf16[1,128,512]{2,1,0:T(8,128)(2,1)}, u32[]{:S(2)}) copy-start(bf16[1,128,512]{2,1,0:T(8,128)(2,1)} %get-tuple-element.5) | copy-start | bytes 393220

commit v4 on v3

--- a/solution.py
+++ b/solution.py
@@ -10,16 +10,17 @@
 AXES = ("bricks", "grp")
 
 
-def window_matrix(shifts, kinds):
-    table = np.zeros((4, 2, 64, len(shifts), 2, 64), np.float32)
-    for w, (b, c) in enumerate(shifts):
+def shift_matrix(dim):
+    table = np.zeros((2, 2, 8, 8, 2, 2, 8, 8), np.float32)
+    for w, shift in enumerate((-1, 1)):
         for y in range(8):
             for z in range(8):
-                yy, zz = y + b, z + c
-                kind = (1 if not 0 <= yy < 8 else 0) + (2 if not 0 <= zz < 8 else 0)
+                at = [y, z]
+                at[dim] += shift
+                kind = 0 if 0 <= at[dim] < 8 else 1
                 for half in range(2):
-                    table[kind, half, (yy % 8) * 8 + zz % 8, w, half, y * 8 + z] = 1.0
-    return table[kinds].reshape(128 * len(kinds), 128 * len(shifts)).astype(jnp.bfloat16)
+                    table[kind, half, at[0] % 8, at[1] % 8, w, half, y, z] = 1.0
+    return table.reshape(256, 256).astype(jnp.bfloat16)
 
 
 def stride_matrix():
@@ -68,21 +69,23 @@
     return lax.dot_general(eye, x, dims, preferred_element_type=jnp.float32).astype(jnp.bfloat16)
 
 
-def stack(centre, halo_y, halo_z, corner, side_y, side_z, side_yz):
-    tiles = centre.shape[0] // 64
-    pair_y = dot(jnp.concatenate([centre, halo_y], axis=1), side_y).astype(jnp.bfloat16)
-    pair_z = dot(jnp.concatenate([centre, halo_z], axis=1), side_z).astype(jnp.bfloat16)
-    four = jnp.concatenate([centre, halo_y, halo_z, corner], axis=1)
-    quad = dot(four, side_yz).astype(jnp.bfloat16)
-    order = [
-        (quad, 0), (pair_y, 0), (quad, 1), (pair_z, 0), (centre, 0),
-        (pair_z, 1), (quad, 2), (pair_y, 1), (quad, 3),
-    ]
+def stack(centre, halo_y, halo_z, corner, side_y, side_z):
+    rows = centre.shape[0]
+    tiles = rows // 64
+    own = jnp.concatenate([centre, halo_y], axis=1)
+    rim = jnp.concatenate([halo_z, corner], axis=1)
+    moved = dot(jnp.concatenate([own, rim], axis=0), side_y).astype(jnp.bfloat16)
+    planes = [moved[:rows, :128], centre, moved[:rows, 128:]]
+    rims = [moved[rows:, :128], halo_z, moved[rows:, 128:]]
+    pairs = [jnp.concatenate([a, b], axis=1) for a, b in zip(planes, rims)]
+    turned = dot(jnp.concatenate(pairs, axis=0), side_z).astype(jnp.bfloat16)
+    order = []
+    for b in range(3):
+        part = turned[rows * b : rows * (b + 1)]
+        order += [part[:, :128], planes[b], part[:, 128:]]
     return jnp.concatenate(
         [
-            jnp.concatenate(
-                [m[64 * p : 64 * p + 64, 128 * w : 128 * w + 128] for m, w in order], axis=0
-            )
+            jnp.concatenate([m[64 * p : 64 * p + 64] for m in order], axis=0)
             for p in range(tiles)
         ],
         axis=1,
@@ -106,11 +109,11 @@
 
 def kernel(
     occ_hbm, gain_hbm, feat_hbm, map_hbm, near_hbm, weight_hbm, side_y_hbm, side_z_hbm,
-    side_yz_hbm, perm_hbm, stride_hbm, shift_hbm, bias_hbm,
-    fine_hbm, coarse_hbm,
+    perm_hbm, stride_hbm, shift_hbm, bias_hbm,
+    fine, keys, keys_in, octs, octs_in,
     occ_ref, gain_ref, feat, map_ref, near_ref, weight, side_y, side_z,
-    side_yz, perm, stride, shift_ref, bias_ref,
-    act, lower, upper, conv, fine, coarse, weight_t, keys, keys_in, octs, octs_in,
+    perm, stride, shift_ref, bias_ref,
+    act, lower, upper, conv, weight_t,
     local_sem, send_sem, recv_sem,
 ):
     count = feat.shape[0]
@@ -129,7 +132,7 @@
             [
                 (occ_hbm, occ_ref), (gain_hbm, gain_ref), (feat_hbm, feat), (map_hbm, map_ref),
                 (near_hbm, near_ref), (weight_hbm, weight), (side_y_hbm, side_y),
-                (side_z_hbm, side_z), (side_yz_hbm, side_yz), (perm_hbm, perm),
+                (side_z_hbm, side_z), (perm_hbm, perm),
                 (stride_hbm, stride), (shift_hbm, shift_ref), (bias_hbm, bias_ref),
             ]
         )
@@ -171,7 +174,7 @@
         scale = lax.rsqrt(jnp.mean(values * values, axis=0, keepdims=True) + norm_eps)
         normed = values * scale * gain
         mask = occ_ref[pl.ds(i, 1), :].astype(jnp.float32)
-        act[i] = (normed / (1.0 + jnp.exp(-normed)) * mask).astype(jnp.bfloat16)
+        act[i] = (normed * (mask * 0.5) * (1.0 + jnp.tanh(0.5 * normed))).astype(jnp.bfloat16)
         return carry
 
     lax.fori_loop(0, count, activate_one, 0, unroll=2)
@@ -233,7 +236,7 @@
             jnp.concatenate([m[:, 128 * p : 128 * p + 128] for p in range(4)], axis=0)
             for m in wide
         ]
-        stacked = stack(*tall, side_y[...], side_z[...], side_yz[...])
+        stacked = stack(*tall, side_y[...], side_z[...])
         product = dot(weight_t[...], stacked)
 
         def part(dx, p):
@@ -264,7 +267,6 @@
     step = count // 2
     outside = jnp.concatenate([weight_t[0:64], weight_t[128:192]], axis=0)
     sent = []
-    stores = []
     for g in range(2):
         group = pl.ds(g * step, step)
         tall = [[], [], [], []]
@@ -278,7 +280,7 @@
             for into, piece in zip(tall, edge):
                 into.append(piece)
         tall = [jnp.concatenate(m, axis=0) for m in tall]
-        stacked = stack(*tall, side_y[...], side_z[...], side_yz[...])
+        stacked = stack(*tall, side_y[...], side_z[...])
         product = dot(outside, stacked)
         for n in range(step):
             i = g * step + n
@@ -295,12 +297,6 @@
                 axis=1,
             )
             fine[i] = (mask * (summed + ends)).astype(jnp.bfloat16)
-        store = pltpu.make_async_copy(
-            fine.at[group], fine_hbm.at[group], local_sem.at[len(loads) + g]
-        )
-        store.start()
-        stores.append(store)
-
         ordered = dot(fine[group].reshape(step * 64, 512), perm[...])
         columns = []
         for j in range(0, step, 2):
@@ -317,16 +313,23 @@
         swap.start()
         sent.append(swap)
 
-    total = place(keys[...], octs[0], octs[1], device, count)
     swap_keys.wait()
     for swap in sent:
         swap.wait()
+
+
+def finish(fine, keys, keys_in, octs, octs_in, fine_hbm, coarse_hbm, coarse, sem):
+    count = fine.shape[0]
+    device = lax.axis_index("bricks") * lax.axis_size("grp") + lax.axis_index("grp")
+    store = pltpu.make_async_copy(fine, fine_hbm, sem.at[0])
+    store.start()
+    total = place(keys[...], octs[0], octs[1], device, count)
     total = total + place(keys_in[...], octs_in[0], octs_in[1], device, count)
     coarse[0] = total.astype(jnp.bfloat16)
-    store = pltpu.make_async_copy(coarse, coarse_hbm, local_sem.at[len(loads) + 2])
-    store.start()
-    for store in stores + [store]:
-        store.wait()
+    last = pltpu.make_async_copy(coarse, coarse_hbm, sem.at[1])
+    last.start()
+    store.wait()
+    last.wait()
 
 
 def shards(
@@ -335,18 +338,20 @@
 ):
     count = features.shape[0]
     bf16 = jnp.bfloat16
-    hbm = pl.BlockSpec(memory_space=pl.ANY)
-    side_y = window_matrix([(-1, 0), (1, 0)], [0, 1])
-    side_z = window_matrix([(0, -1), (0, 1)], [0, 2])
-    side_yz = window_matrix([(-1, -1), (-1, 1), (1, -1), (1, 1)], [0, 1, 2, 3])
-    return pl.pallas_call(
+    hbm = pl.BlockSpec(memory_space=pltpu.HBM)
+    vmem = pl.BlockSpec(memory_space=pltpu.VMEM)
+    side_y, side_z = shift_matrix(0), shift_matrix(1)
+    found = pl.pallas_call(
         kernel,
         out_shape=(
             jax.ShapeDtypeStruct(features.shape, bf16),
-            jax.ShapeDtypeStruct((1, 128, 512), bf16),
+            jax.ShapeDtypeStruct((count, 128), jnp.int32),
+            jax.ShapeDtypeStruct((count, 128), jnp.int32),
+            jax.ShapeDtypeStruct((2, 128, 32 * count), bf16),
+            jax.ShapeDtypeStruct((2, 128, 32 * count), bf16),
         ),
-        in_specs=[hbm] * 13,
-        out_specs=(hbm, hbm),
+        in_specs=[hbm] * 12,
+        out_specs=(vmem,) * 5,
         scratch_shapes=[
             pltpu.VMEM((count, 512), jnp.int32),
             pltpu.VMEM((1, 64), jnp.float32),
@@ -357,7 +362,6 @@
             pltpu.VMEM((256, 256), bf16),
             pltpu.VMEM((256, 256), bf16),
             pltpu.VMEM((512, 512), bf16),
-            pltpu.VMEM((512, 512), bf16),
             pltpu.VMEM((512, 128), bf16),
             pltpu.VMEM((1, 64), jnp.float32),
             pltpu.VMEM((1, 128), jnp.float32),
@@ -365,26 +369,35 @@
             pltpu.VMEM((count + 1, 64, 128), bf16),
             pltpu.VMEM((count + 1, 64, 128), bf16),
             pltpu.VMEM((count, 64, 512), jnp.float32),
-            pltpu.VMEM((count, 64, 512), bf16),
-            pltpu.VMEM((1, 128, 512), bf16),
             pltpu.VMEM((192, 576), bf16),
-            pltpu.VMEM((count, 128), jnp.int32),
-            pltpu.VMEM((count, 128), jnp.int32),
-            pltpu.VMEM((2, 128, 32 * count), bf16),
-            pltpu.VMEM((2, 128, 32 * count), bf16),
             pltpu.SemaphoreType.DMA((16,)),
             pltpu.SemaphoreType.DMA((5,)),
             pltpu.SemaphoreType.DMA((5,)),
         ],
         compiler_params=pltpu.CompilerParams(
-            collective_id=0, has_side_effects=True, vmem_limit_bytes=63 * 1024 * 1024
+            collective_id=0, has_side_effects=True, vmem_limit_bytes=32 * 1024 * 1024
         ),
         name="bricks",
-    )(
-        occupancy, norm_gain[None], features, coarse_map[None], neighbours,
-        conv_weight.reshape(1728, 64), side_y, side_z, side_yz, stride_matrix(),
-        stride_weight.reshape(512, 128), time_shift[None], coarse_bias[None],
-    )
+    )(*[
+        pltpu.with_memory_space_constraint(x, pltpu.HBM)
+        for x in (
+            occupancy, norm_gain[None], features, coarse_map[None], neighbours,
+            conv_weight.reshape(1728, 64), side_y, side_z, stride_matrix(),
+            stride_weight.reshape(512, 128), time_shift[None], coarse_bias[None],
+        )
+    ])
+    return pl.pallas_call(
+        finish,
+        out_shape=(
+            jax.ShapeDtypeStruct(features.shape, bf16),
+            jax.ShapeDtypeStruct((1, 128, 512), bf16),
+        ),
+        in_specs=[vmem] * 5,
+        out_specs=(hbm, hbm),
+        scratch_shapes=[pltpu.VMEM((1, 128, 512), bf16), pltpu.SemaphoreType.DMA((2,))],
+        compiler_params=pltpu.CompilerParams(vmem_limit_bytes=16 * 1024 * 1024),
+        name="finish",
+    )(*found)
 
 
 def solution(mesh):

time: 18.1 us -> 16.3 us (0.901)
  local copies, waits for them, and re-layouts: 2.56 us -> 0 us
  Pallas kernels: 14.6 us -> 15.5 us
    unnamed x4 -> x0, local copies, waits for them, and re-layouts: 2.56 us -> none
    pallas_call x0 -> x1, Pallas kernels: none -> 1 us  [shards(): pl.pallas_call(finish, out_shape=(jax.ShapeDtypeStruct(features.shape, bf...]
where the time goes in v4:
time: 16.3 us; the launch traced here: 16.1 us
  Pallas kernels  15.5 us (95%)
  between operations  0.64 us (4%)
    pallas_call x1, Pallas kernels, shards(): pl.pallas_call(kernel, out_shape=(jax.ShapeDtypeStruct(features.shape, bf...  14.5 us
    pallas_call x1, Pallas kernels, shards(): pl.pallas_call(finish, out_shape=(jax.ShapeDtypeStruct(features.shape, bf...  1 us

profile of v4, /device:TPU:5, one launch (start us, length us, event | category | flops | bytes accessed | tf_op | source)
XLA Modules:
  0.0 16.1 jit_solution(2953934583605910530)
XLA Ops:
  0.6 14.5 %bricks.1 = (bf16[8,64,512]{2,1,0:T(8,128)(2,1)S(1)}, s32[8,128]{1,0:T(8,128)S(1)}, s32[8,128]{1,0:T(8,128)S(1)}, bf16[2,128,256]{2,1,0:T(8,128)(2,1)S(1)}, bf16[2,128,256]{2,1,0:T(8,128)(2,1)S(1)}) custom-call(s32[8,512]{1,0:T(8,128)} %occ_hbm.1, f32[1,64]{1,0:T(1,128)} %bitcast.8, bf16[8,64,512]{2,1,0:T(8,128)(2,1)} %feat_hbm.1, s32[1,8]{1,0:T(1,128)} %bitcast.9, ...), custom_call_target="tpu_custom_call" | custom-call | tf_op jit(solution)/shard_map/bricks/pallas_call | solution.py:344
  15.1 1.0 %finish.1 = (bf16[8,64,512]{2,1,0:T(8,128)(2,1)}, bf16[1,128,512]{2,1,0:T(8,128)(2,1)}) custom-call(bf16[8,64,512]{2,1,0:T(8,128)(2,1)S(1)} %get-tuple-element.7.fine, s32[8,128]{1,0:T(8,128)S(1)} %get-tuple-element.8.keys, s32[8,128]{1,0:T(8,128)S(1)} %get-tuple-element.9.keys_in, bf16[2,128,256]{2,1,0:T(8,128)(2,1)S(1)} %get-tuple-element.10.octs, ...), custom_call_target="tpu_custom_call" | custom-call | tf_op jit(solution)/shard_map/finish/pallas_call | solution.py:389

commit v5 on v4

--- a/solution.py
+++ b/solution.py
@@ -8,19 +8,6 @@
 
 norm_eps = 1e-06
 AXES = ("bricks", "grp")
-
-
-def shift_matrix(dim):
-    table = np.zeros((2, 2, 8, 8, 2, 2, 8, 8), np.float32)
-    for w, shift in enumerate((-1, 1)):
-        for y in range(8):
-            for z in range(8):
-                at = [y, z]
-                at[dim] += shift
-                kind = 0 if 0 <= at[dim] < 8 else 1
-                for half in range(2):
-                    table[kind, half, at[0] % 8, at[1] % 8, w, half, y, z] = 1.0
-    return table.reshape(256, 256).astype(jnp.bfloat16)
 
 
 def stride_matrix():
@@ -50,14 +37,16 @@
     return jnp.dot(a, b, preferred_element_type=jnp.float32)
 
 
-def halos(fetch, masks):
-    low_y, low_z = masks
-    high_y, high_z = 1 - low_y, 1 - low_z
-    halo_y = fetch(1, 0) * low_y + fetch(-1, 0) * high_y
-    halo_z = fetch(0, 1) * low_z + fetch(0, -1) * high_z
-    near = fetch(1, 1) * low_z + fetch(1, -1) * high_z
-    far = fetch(-1, 1) * low_z + fetch(-1, -1) * high_z
-    return halo_y, halo_z, near * low_y + far * high_y
+def halos(fetch, y_low, z_low):
+    halo_y = jnp.where(y_low, fetch(1, 0), fetch(-1, 0))
+    halo_z = jnp.where(z_low, fetch(0, 1), fetch(0, -1))
+    near = jnp.where(z_low, fetch(1, 1), fetch(1, -1))
+    far = jnp.where(z_low, fetch(-1, 1), fetch(-1, -1))
+    return halo_y, halo_z, jnp.where(y_low, near, far)
+
+
+def turn(x, by):
+    return pltpu.roll(x, by % 128, 1)
 
 
 def flipped(x):
@@ -69,27 +58,21 @@
     return lax.dot_general(eye, x, dims, preferred_element_type=jnp.float32).astype(jnp.bfloat16)
 
 
-def stack(centre, halo_y, halo_z, corner, side_y, side_z):
-    rows = centre.shape[0]
-    tiles = rows // 64
-    own = jnp.concatenate([centre, halo_y], axis=1)
-    rim = jnp.concatenate([halo_z, corner], axis=1)
-    moved = dot(jnp.concatenate([own, rim], axis=0), side_y).astype(jnp.bfloat16)
-    planes = [moved[:rows, :128], centre, moved[:rows, 128:]]
-    rims = [moved[rows:, :128], halo_z, moved[rows:, 128:]]
-    pairs = [jnp.concatenate([a, b], axis=1) for a, b in zip(planes, rims)]
-    turned = dot(jnp.concatenate(pairs, axis=0), side_z).astype(jnp.bfloat16)
+def stack(own, halo_y, halo_z, corner, ends):
+    y_first, y_last, z_first, z_last = ends
+
+    def along_y(x, halo):
+        far = turn(halo, 64)
+        return (
+            turn(jnp.where(y_last, far, x), 8), x, turn(jnp.where(y_first, far, x), -8),
+        )
+
     order = []
-    for b in range(3):
-        part = turned[rows * b : rows * (b + 1)]
-        order += [part[:, :128], planes[b], part[:, 128:]]
-    return jnp.concatenate(
-        [
-            jnp.concatenate([m[64 * p : 64 * p + 64] for m in order], axis=0)
-            for p in range(tiles)
-        ],
-        axis=1,
-    )
+    for plane, rim in zip(along_y(own, halo_y), along_y(halo_z, corner)):
+        order.append(turn(jnp.where(z_last, turn(rim, -8), plane), 1))
+        order.append(plane)
+        order.append(turn(jnp.where(z_first, turn(rim, 8), plane), -1))
+    return jnp.concatenate(order, axis=0)
 
 
 def place(keys, near, far, coarse, count):
@@ -108,11 +91,11 @@
 
 
 def kernel(
-    occ_hbm, gain_hbm, feat_hbm, map_hbm, near_hbm, weight_hbm, side_y_hbm, side_z_hbm,
-    perm_hbm, stride_hbm, shift_hbm, bias_hbm,
+    occ_hbm, gain_hbm, feat_hbm, map_hbm, near_hbm, weight_hbm, perm_hbm,
+    stride_hbm, shift_hbm, bias_hbm,
     fine, keys, keys_in, octs, octs_in,
-    occ_ref, gain_ref, feat, map_ref, near_ref, weight, side_y, side_z,
-    perm, stride, shift_ref, bias_ref,
+    occ_ref, gain_ref, feat, map_ref, near_ref, weight, perm,
+    stride, shift_ref, bias_ref,
     act, lower, upper, conv, weight_t,
     local_sem, send_sem, recv_sem,
 ):
@@ -131,8 +114,7 @@
         for n, (src, dst) in enumerate(
             [
                 (occ_hbm, occ_ref), (gain_hbm, gain_ref), (feat_hbm, feat), (map_hbm, map_ref),
-                (near_hbm, near_ref), (weight_hbm, weight), (side_y_hbm, side_y),
-                (side_z_hbm, side_z), (perm_hbm, perm),
+                (near_hbm, near_ref), (weight_hbm, weight), (perm_hbm, perm),
                 (stride_hbm, stride), (shift_hbm, shift_ref), (bias_hbm, bias_ref),
             ]
         )
@@ -215,12 +197,11 @@
     for a in range(3):
         weight_t[64 * a : 64 * a + 64] = flipped(weight[576 * a : 576 * a + 576])
 
-    lane = lax.broadcasted_iota(jnp.int32, (64, 512), 1)
-    low_y = jnp.where(lane % 64 < 32, 1.0, 0.0).astype(jnp.bfloat16)
-    low_z = jnp.where(lane % 8 < 4, 1.0, 0.0).astype(jnp.bfloat16)
-    half = lax.broadcasted_iota(jnp.int32, (64, 128), 1) < 64
-    first = jnp.where(half, 1.0, 0.0).astype(jnp.bfloat16)
-    second = 1 - first
+    lane = lax.broadcasted_iota(jnp.int32, (64, 128), 1)
+    half = lane < 64
+    y_low = (lane & 63) < 32
+    z_low = (lane & 7) < 4
+    marks = ((lane & 63) < 8, (lane & 63) >= 56, (lane & 7) == 0, (lane & 7) == 7)
 
     def row(i, dx, dy, dz):
         target = near_ref[i, offset(dx, dy, dz)]
@@ -228,16 +209,19 @@
         return jnp.where(target < 0, count, local)
 
     def middle(i, carry):
-        def own(dy, dz):
-            return act[row(i, 0, dy, dz)]
-
-        wide = (act[i],) + halos(own, (low_y, low_z))
-        tall = [
-            jnp.concatenate([m[:, 128 * p : 128 * p + 128] for p in range(4)], axis=0)
-            for m in wide
-        ]
-        stacked = stack(*tall, side_y[...], side_z[...])
-        product = dot(weight_t[...], stacked)
+        rows = {
+            (dy, dz): row(i, 0, dy, dz)
+            for dy in (-1, 0, 1) for dz in (-1, 0, 1) if (dy, dz) != (0, 0)
+        }
+        columns = []
+        for p in range(4):
+
+            def own(dy, dz):
+                return act[rows[dy, dz], :, 128 * p : 128 * p + 128]
+
+            tile = act[i, :, 128 * p : 128 * p + 128]
+            columns.append(stack(tile, *halos(own, y_low, z_low), marks))
+        product = dot(weight_t[...], jnp.concatenate(columns, axis=1))
 
         def part(dx, p):
             if not 0 <= p < 4:
@@ -269,18 +253,15 @@
     sent = []
     for g in range(2):
         group = pl.ds(g * step, step)
-        tall = [[], [], [], []]
+        tall = []
         for n in range(step):
             i = g * step + n
 
             def outer(dy, dz):
-                return upper[row(i, 1, dy, dz)] * first + lower[row(i, -1, dy, dz)] * second
-
-            edge = (outer(0, 0),) + halos(outer, (low_y[:, :128], low_z[:, :128]))
-            for into, piece in zip(tall, edge):
-                into.append(piece)
-        tall = [jnp.concatenate(m, axis=0) for m in tall]
-        stacked = stack(*tall, side_y[...], side_z[...])
+                return jnp.where(half, upper[row(i, 1, dy, dz)], lower[row(i, -1, dy, dz)])
+
+            tall.append(stack(outer(0, 0), *halos(outer, y_low, z_low), marks))
+        stacked = jnp.concatenate(tall, axis=1)
         product = dot(outside, stacked)
         for n in range(step):
             i = g * step + n
@@ -340,7 +321,6 @@
     bf16 = jnp.bfloat16
     hbm = pl.BlockSpec(memory_space=pltpu.HBM)
     vmem = pl.BlockSpec(memory_space=pltpu.VMEM)
-    side_y, side_z = shift_matrix(0), shift_matrix(1)
     found = pl.pallas_call(
         kernel,
         out_shape=(
@@ -350,7 +330,7 @@
             jax.ShapeDtypeStruct((2, 128, 32 * count), bf16),
             jax.ShapeDtypeStruct((2, 128, 32 * count), bf16),
         ),
-        in_specs=[hbm] * 12,
+        in_specs=[hbm] * 10,
         out_specs=(vmem,) * 5,
         scratch_shapes=[
             pltpu.VMEM((count, 512), jnp.int32),
@@ -359,8 +339,6 @@
             pltpu.VMEM((1, count), jnp.int32),
             pltpu.SMEM((count, 26), jnp.int32),
             pltpu.VMEM((1728, 64), bf16),
-            pltpu.VMEM((256, 256), bf16),
-            pltpu.VMEM((256, 256), bf16),
             pltpu.VMEM((512, 512), bf16),
             pltpu.VMEM((512, 128), bf16),
             pltpu.VMEM((1, 64), jnp.float32),
@@ -382,7 +360,7 @@
         pltpu.with_memory_space_constraint(x, pltpu.HBM)
         for x in (
             occupancy, norm_gain[None], features, coarse_map[None], neighbours,
-            conv_weight.reshape(1728, 64), side_y, side_z, stride_matrix(),
+            conv_weight.reshape(1728, 64), stride_matrix(),
             stride_weight.reshape(512, 128), time_shift[None], coarse_bias[None],
         )
     ])

time: 16.3 us -> 16.5 us (1.012)
  no operation moved by 1% of the time
where the time goes in v5:
time: 16.5 us; the launch traced here: 16.2 us
  Pallas kernels  15.6 us (95%)
  between operations  0.64 us (4%)
    pallas_call x1, Pallas kernels, shards(): pl.pallas_call(kernel, out_shape=(jax.ShapeDtypeStruct(features.shape, bf...  14.6 us
    pallas_call x1, Pallas kernels, shards(): pl.pallas_call(finish, out_shape=(jax.ShapeDtypeStruct(features.shape, bf...  1 us

profile of v5, /device:TPU:5, one launch (start us, length us, event | category | flops | bytes accessed | tf_op | source)
XLA Modules:
  0.0 16.2 jit_solution(8188812648023694005)
XLA Ops:
  0.6 14.6 %bricks.1 = (bf16[8,64,512]{2,1,0:T(8,128)(2,1)S(1)}, s32[8,128]{1,0:T(8,128)S(1)}, s32[8,128]{1,0:T(8,128)S(1)}, bf16[2,128,256]{2,1,0:T(8,128)(2,1)S(1)}, bf16[2,128,256]{2,1,0:T(8,128)(2,1)S(1)}) custom-call(s32[8,512]{1,0:T(8,128)} %occ_hbm.1, f32[1,64]{1,0:T(1,128)} %bitcast.8, bf16[8,64,512]{2,1,0:T(8,128)(2,1)} %feat_hbm.1, s32[1,8]{1,0:T(1,128)} %bitcast.9, ...), custom_call_target="tpu_custom_call" | custom-call | tf_op jit(solution)/shard_map/bricks/pallas_call | solution.py:324
  15.2 1.0 %finish.1 = (bf16[8,64,512]{2,1,0:T(8,128)(2,1)}, bf16[1,128,512]{2,1,0:T(8,128)(2,1)}) custom-call(bf16[8,64,512]{2,1,0:T(8,128)(2,1)S(1)} %get-tuple-element.7.fine, s32[8,128]{1,0:T(8,128)S(1)} %get-tuple-element.8.keys, s32[8,128]{1,0:T(8,128)S(1)} %get-tuple-element.9.keys_in, bf16[2,128,256]{2,1,0:T(8,128)(2,1)S(1)} %get-tuple-element.10.octs, ...), custom_call_target="tpu_custom_call" | custom-call | tf_op jit(solution)/shard_map/finish/pallas_call | solution.py:367

commit v6 on v5

--- a/solution.py
+++ b/solution.py
@@ -96,7 +96,7 @@
     fine, keys, keys_in, octs, octs_in,
     occ_ref, gain_ref, feat, map_ref, near_ref, weight, perm,
     stride, shift_ref, bias_ref,
-    act, lower, upper, conv, weight_t,
+    act, lower, upper, conv, weight_t, rising, falling, risen, fallen,
     local_sem, send_sem, recv_sem,
 ):
     count = feat.shape[0]
@@ -113,8 +113,12 @@
         pltpu.make_async_copy(src, dst, local_sem.at[n])
         for n, (src, dst) in enumerate(
             [
-                (occ_hbm, occ_ref), (gain_hbm, gain_ref), (feat_hbm, feat), (map_hbm, map_ref),
-                (near_hbm, near_ref), (weight_hbm, weight), (perm_hbm, perm),
+                (occ_hbm, occ_ref), (gain_hbm, gain_ref),
+                (feat_hbm.at[:, :, pl.ds(0, 128)], feat.at[:, :, pl.ds(0, 128)]),
+                (feat_hbm.at[:, :, pl.ds(384, 128)], feat.at[:, :, pl.ds(384, 128)]),
+                (map_hbm, map_ref), (weight_hbm, weight),
+                (feat_hbm.at[:, :, pl.ds(128, 256)], feat.at[:, :, pl.ds(128, 256)]),
+                (near_hbm, near_ref), (perm_hbm, perm),
                 (stride_hbm, stride), (shift_hbm, shift_ref), (bias_hbm, bias_ref),
             ]
         )
@@ -141,29 +145,33 @@
 
     @pl.when(jnp.logical_not(has_left))
     def _():
-        lower[0:count] = jnp.zeros((count, 64, 128), jnp.bfloat16)
+        risen[...] = jnp.zeros(risen.shape, jnp.bfloat16)
 
     @pl.when(jnp.logical_not(has_right))
     def _():
-        upper[0:count] = jnp.zeros((count, 64, 128), jnp.bfloat16)
-
-    for load in loads[:3]:
+        fallen[...] = jnp.zeros(fallen.shape, jnp.bfloat16)
+
+    for load in loads[:4]:
         load.wait()
     gain = column(gain_ref[...])
-
-    def activate_one(i, carry):
-        values = feat[i].astype(jnp.float32)
+    lane = lax.broadcasted_iota(jnp.int32, (64, 128), 1)
+    half = lane < 64
+
+    def activate(i, start, size):
+        lanes = slice(start, start + size)
+        values = feat[i, :, lanes].astype(jnp.float32)
         scale = lax.rsqrt(jnp.mean(values * values, axis=0, keepdims=True) + norm_eps)
         normed = values * scale * gain
-        mask = occ_ref[pl.ds(i, 1), :].astype(jnp.float32)
-        act[i] = (normed * (mask * 0.5) * (1.0 + jnp.tanh(0.5 * normed))).astype(jnp.bfloat16)
-        return carry
-
-    lax.fori_loop(0, count, activate_one, 0, unroll=2)
-    loads[3].wait()
-    keys[...] = jnp.broadcast_to(
-        column(map_ref[...].astype(jnp.float32)).astype(jnp.int32), keys.shape
-    )
+        mask = occ_ref[pl.ds(i, 1), lanes].astype(jnp.float32)
+        result = (normed * (mask * 0.5) * (1.0 + jnp.tanh(0.5 * normed))).astype(jnp.bfloat16)
+        act[i, :, lanes] = result
+        return result
+
+    for j in range(count // 2):
+        left, right = activate(2 * j, 0, 128), activate(2 * j + 1, 0, 128)
+        falling[j] = jnp.where(half, left, turn(right, 64))
+        left, right = activate(2 * j, 384, 128), activate(2 * j + 1, 384, 128)
+        rising[j] = jnp.where(half, turn(left, 64), right)
 
     def remote(n, src, dst, other):
         return pltpu.make_async_remote_copy(
@@ -171,9 +179,8 @@
             device_id=coords(other), device_id_type=pl.DeviceIdType.MESH,
         )
 
-    bricks = pl.ds(0, count)
-    rise = remote(0, act.at[bricks, :, pl.ds(384, 128)], lower.at[bricks], device + 1)
-    fall = remote(1, act.at[bricks, :, pl.ds(0, 128)], upper.at[bricks], device - 1)
+    rise = remote(0, rising, risen, device + 1)
+    fall = remote(1, falling, fallen, device - 1)
     mate = device + 1 - 2 * (device % 2)
     swap_keys = remote(2, keys, keys_in, mate)
 
@@ -187,9 +194,13 @@
     def _():
         fall.start()
 
+    loads[4].wait()
+    keys[...] = jnp.broadcast_to(
+        column(map_ref[...].astype(jnp.float32)).astype(jnp.int32), keys.shape
+    )
     swap_keys.start()
 
-    for load in loads[4:]:
+    for load in loads[5:]:
         load.wait()
     shift = column(shift_ref[...])
     bias = column(bias_ref[...])
@@ -197,8 +208,11 @@
     for a in range(3):
         weight_t[64 * a : 64 * a + 64] = flipped(weight[576 * a : 576 * a + 576])
 
-    lane = lax.broadcasted_iota(jnp.int32, (64, 128), 1)
-    half = lane < 64
+    def activate_rest(i, carry):
+        activate(i, 128, 256)
+        return carry
+
+    lax.fori_loop(0, count, activate_rest, 0, unroll=4)
     y_low = (lane & 63) < 32
     z_low = (lane & 7) < 4
     marks = ((lane & 63) < 8, (lane & 63) >= 56, (lane & 7) == 0, (lane & 7) == 7)
@@ -247,6 +261,12 @@
     def _():
         fall.wait_recv()
         rise.wait_send()
+
+    for j in range(count // 2):
+        lower[2 * j] = turn(risen[j], 64)
+        lower[2 * j + 1] = risen[j]
+        upper[2 * j] = fallen[j]
+        upper[2 * j + 1] = turn(fallen[j], 64)
 
     step = count // 2
     outside = jnp.concatenate([weight_t[0:64], weight_t[128:192]], axis=0)
@@ -348,6 +368,10 @@
             pltpu.VMEM((count + 1, 64, 128), bf16),
             pltpu.VMEM((count, 64, 512), jnp.float32),
             pltpu.VMEM((192, 576), bf16),
+            pltpu.VMEM((count // 2, 64, 128), bf16),
+            pltpu.VMEM((count // 2, 64, 128), bf16),
+            pltpu.VMEM((count // 2, 64, 128), bf16),
+            pltpu.VMEM((count // 2, 64, 128), bf16),
             pltpu.SemaphoreType.DMA((16,)),
             pltpu.SemaphoreType.DMA((5,)),
             pltpu.SemaphoreType.DMA((5,)),

time: 16.5 us -> 16.9 us (1.024)
  Pallas kernels: 15.6 us -> 16 us
    pallas_call x1, Pallas kernels: 14.6 us -> 15 us  [shards(): pl.pallas_call(kernel, out_shape=(jax.ShapeDtypeStruct(features.shape, bf...]
where the time goes in v6:
time: 16.9 us; the launch traced here: 16.6 us
  Pallas kernels  16 us (95%)
  between operations  0.64 us (4%)
    pallas_call x1, Pallas kernels, shards(): pl.pallas_call(kernel, out_shape=(jax.ShapeDtypeStruct(features.shape, bf...  15 us
    pallas_call x1, Pallas kernels, shards(): pl.pallas_call(finish, out_shape=(jax.ShapeDtypeStruct(features.shape, bf...  1 us

profile of v6, /device:TPU:5, one launch (start us, length us, event | category | flops | bytes accessed | tf_op | source)
XLA Modules:
  0.0 16.6 jit_solution(6099509699076686976)
XLA Ops:
  0.6 15.0 %bricks.1 = (bf16[8,64,512]{2,1,0:T(8,128)(2,1)S(1)}, s32[8,128]{1,0:T(8,128)S(1)}, s32[8,128]{1,0:T(8,128)S(1)}, bf16[2,128,256]{2,1,0:T(8,128)(2,1)S(1)}, bf16[2,128,256]{2,1,0:T(8,128)(2,1)S(1)}) custom-call(s32[8,512]{1,0:T(8,128)} %occ_hbm.1, f32[1,64]{1,0:T(1,128)} %bitcast.8, bf16[8,64,512]{2,1,0:T(8,128)(2,1)} %feat_hbm.1, s32[1,8]{1,0:T(1,128)} %bitcast.9, ...), custom_call_target="tpu_custom_call" | custom-call | tf_op jit(solution)/shard_map/bricks/pallas_call | solution.py:344
  15.6 1.0 %finish.1 = (bf16[8,64,512]{2,1,0:T(8,128)(2,1)}, bf16[1,128,512]{2,1,0:T(8,128)(2,1)}) custom-call(bf16[8,64,512]{2,1,0:T(8,128)(2,1)S(1)} %get-tuple-element.7.fine, s32[8,128]{1,0:T(8,128)S(1)} %get-tuple-element.8.keys, s32[8,128]{1,0:T(8,128)S(1)} %get-tuple-element.9.keys_in, bf16[2,128,256]{2,1,0:T(8,128)(2,1)S(1)} %get-tuple-element.10.octs, ...), custom_call_target="tpu_custom_call" | custom-call | tf_op jit(solution)/shard_map/finish/pallas_call | solution.py:391

commit v7 on v6

--- a/solution.py
+++ b/solution.py
@@ -8,6 +8,16 @@
 
 norm_eps = 1e-06
 AXES = ("bricks", "grp")
+
+
+def side_matrix():
+    table = np.zeros((2, 16, 8, 2, 16, 8), np.float32)
+    for w, shift in enumerate((-1, 1)):
+        for z in range(8):
+            kind = 0 if 0 <= z + shift < 8 else 1
+            for line in range(16):
+                table[kind, line, (z + shift) % 8, w, line, z] = 1.0
+    return table.reshape(256, 256).astype(jnp.bfloat16)
 
 
 def stride_matrix():
@@ -58,8 +68,8 @@
     return lax.dot_general(eye, x, dims, preferred_element_type=jnp.float32).astype(jnp.bfloat16)
 
 
-def stack(own, halo_y, halo_z, corner, ends):
-    y_first, y_last, z_first, z_last = ends
+def stack(tiles, ends, side):
+    y_first, y_last = ends
 
     def along_y(x, halo):
         far = turn(halo, 64)
@@ -67,12 +77,25 @@
             turn(jnp.where(y_last, far, x), 8), x, turn(jnp.where(y_first, far, x), -8),
         )
 
-    order = []
-    for plane, rim in zip(along_y(own, halo_y), along_y(halo_z, corner)):
-        order.append(turn(jnp.where(z_last, turn(rim, -8), plane), 1))
-        order.append(plane)
-        order.append(turn(jnp.where(z_first, turn(rim, 8), plane), -1))
-    return jnp.concatenate(order, axis=0)
+    planes = []
+    rims = []
+    for own, halo_y, halo_z, corner in tiles:
+        planes.append(along_y(own, halo_y))
+        rims.append(along_y(halo_z, corner))
+    pairs = [
+        jnp.concatenate([plane[b], rim[b]], axis=1)
+        for b in range(3) for plane, rim in zip(planes, rims)
+    ]
+    moved = dot(jnp.concatenate(pairs, axis=0), side).astype(jnp.bfloat16)
+    columns = []
+    for t, plane in enumerate(planes):
+        order = []
+        for b in range(3):
+            at = 64 * (b * len(tiles) + t)
+            part = moved[at : at + 64]
+            order += [part[:, :128], plane[b], part[:, 128:]]
+        columns.append(jnp.concatenate(order, axis=0))
+    return jnp.concatenate(columns, axis=1)
 
 
 def place(keys, near, far, coarse, count):
@@ -91,10 +114,10 @@
 
 
 def kernel(
-    occ_hbm, gain_hbm, feat_hbm, map_hbm, near_hbm, weight_hbm, perm_hbm,
+    occ_hbm, gain_hbm, feat_hbm, map_hbm, near_hbm, weight_hbm, side_hbm, perm_hbm,
     stride_hbm, shift_hbm, bias_hbm,
     fine, keys, keys_in, octs, octs_in,
-    occ_ref, gain_ref, feat, map_ref, near_ref, weight, perm,
+    occ_ref, gain_ref, feat, map_ref, near_ref, weight, side, perm,
     stride, shift_ref, bias_ref,
     act, lower, upper, conv, weight_t, rising, falling, risen, fallen,
     local_sem, send_sem, recv_sem,
@@ -118,7 +141,7 @@
                 (feat_hbm.at[:, :, pl.ds(384, 128)], feat.at[:, :, pl.ds(384, 128)]),
                 (map_hbm, map_ref), (weight_hbm, weight),
                 (feat_hbm.at[:, :, pl.ds(128, 256)], feat.at[:, :, pl.ds(128, 256)]),
-                (near_hbm, near_ref), (perm_hbm, perm),
+                (near_hbm, near_ref), (side_hbm, side), (perm_hbm, perm),
                 (stride_hbm, stride), (shift_hbm, shift_ref), (bias_hbm, bias_ref),
             ]
         )
@@ -215,7 +238,7 @@
     lax.fori_loop(0, count, activate_rest, 0, unroll=4)
     y_low = (lane & 63) < 32
     z_low = (lane & 7) < 4
-    marks = ((lane & 63) < 8, (lane & 63) >= 56, (lane & 7) == 0, (lane & 7) == 7)
+    marks = ((lane & 63) < 8, (lane & 63) >= 56)
 
     def row(i, dx, dy, dz):
         target = near_ref[i, offset(dx, dy, dz)]
@@ -234,8 +257,8 @@
                 return act[rows[dy, dz], :, 128 * p : 128 * p + 128]
 
             tile = act[i, :, 128 * p : 128 * p + 128]
-            columns.append(stack(tile, *halos(own, y_low, z_low), marks))
-        product = dot(weight_t[...], jnp.concatenate(columns, axis=1))
+            columns.append((tile, *halos(own, y_low, z_low)))
+        product = dot(weight_t[...], stack(columns, marks, side[...]))
 
         def part(dx, p):
             if not 0 <= p < 4:
@@ -244,13 +267,13 @@
 
         pieces = []
         for p in range(4):
-            below = pltpu.roll(jnp.where(half, part(-1, p), part(-1, p - 1)), 64, 1)
-            above = pltpu.roll(jnp.where(half, part(1, p + 1), part(1, p)), 64, 1)
-            pieces.append(part(0, p) + below + above)
+            below = jnp.where(half, part(-1, p), part(-1, p - 1))
+            above = jnp.where(half, part(1, p + 1), part(1, p))
+            pieces.append(part(0, p) + turn(below + above, 64))
         conv[i] = jnp.concatenate(pieces, axis=1)
         return carry
 
-    lax.fori_loop(0, count, middle, 0, unroll=2)
+    lax.fori_loop(0, count, middle, 0, unroll=4)
 
     @pl.when(has_left)
     def _():
@@ -280,8 +303,8 @@
             def outer(dy, dz):
                 return jnp.where(half, upper[row(i, 1, dy, dz)], lower[row(i, -1, dy, dz)])
 
-            tall.append(stack(outer(0, 0), *halos(outer, y_low, z_low), marks))
-        stacked = jnp.concatenate(tall, axis=1)
+            tall.append((outer(0, 0), *halos(outer, y_low, z_low)))
+        stacked = stack(tall, marks, side[...])
         product = dot(outside, stacked)
         for n in range(step):
             i = g * step + n
@@ -350,7 +373,7 @@
             jax.ShapeDtypeStruct((2, 128, 32 * count), bf16),
             jax.ShapeDtypeStruct((2, 128, 32 * count), bf16),
         ),
-        in_specs=[hbm] * 10,
+        in_specs=[hbm] * 11,
         out_specs=(vmem,) * 5,
         scratch_shapes=[
             pltpu.VMEM((count, 512), jnp.int32),
@@ -359,6 +382,7 @@
             pltpu.VMEM((1, count), jnp.int32),
             pltpu.SMEM((count, 26), jnp.int32),
             pltpu.VMEM((1728, 64), bf16),
+            pltpu.VMEM((256, 256), bf16),
             pltpu.VMEM((512, 512), bf16),
             pltpu.VMEM((512, 128), bf16),
             pltpu.VMEM((1, 64), jnp.float32),
@@ -384,7 +408,7 @@
         pltpu.with_memory_space_constraint(x, pltpu.HBM)
         for x in (
             occupancy, norm_gain[None], features, coarse_map[None], neighbours,
-            conv_weight.reshape(1728, 64), stride_matrix(),
+            conv_weight.reshape(1728, 64), side_matrix(), stride_matrix(),
             stride_weight.reshape(512, 128), time_shift[None], coarse_bias[None],
         )
     ])

time: 16.9 us -> 15 us (0.89)
  Pallas kernels: 16 us -> 14.1 us
    pallas_call x1, Pallas kernels: 15 us -> 13.1 us  [shards(): pl.pallas_call(kernel, out_shape=(jax.ShapeDtypeStruct(features.shape, bf...]
where the time goes in v7:
time: 15 us; the launch traced here: 14.8 us
  Pallas kernels  14.1 us (94%)
  between operations  0.64 us (4%)
    pallas_call x1, Pallas kernels, shards(): pl.pallas_call(kernel, out_shape=(jax.ShapeDtypeStruct(features.shape, bf...  13.1 us
    pallas_call x1, Pallas kernels, shards(): pl.pallas_call(finish, out_shape=(jax.ShapeDtypeStruct(features.shape, bf...  1 us

profile of v7, /device:TPU:5, one launch (start us, length us, event | category | flops | bytes accessed | tf_op | source)
XLA Modules:
  0.0 14.8 jit_solution(14038196180488750442)
XLA Ops:
  0.6 13.1 %bricks.1 = (bf16[8,64,512]{2,1,0:T(8,128)(2,1)S(1)}, s32[8,128]{1,0:T(8,128)S(1)}, s32[8,128]{1,0:T(8,128)S(1)}, bf16[2,128,256]{2,1,0:T(8,128)(2,1)S(1)}, bf16[2,128,256]{2,1,0:T(8,128)(2,1)S(1)}) custom-call(s32[8,512]{1,0:T(8,128)} %occ_hbm.1, f32[1,64]{1,0:T(1,128)} %bitcast.8, bf16[8,64,512]{2,1,0:T(8,128)(2,1)} %feat_hbm.1, s32[1,8]{1,0:T(1,128)} %bitcast.9, ...), custom_call_target="tpu_custom_call" | custom-call | tf_op jit(solution)/shard_map/bricks/pallas_call | solution.py:367
  13.8 1.0 %finish.1 = (bf16[8,64,512]{2,1,0:T(8,128)(2,1)}, bf16[1,128,512]{2,1,0:T(8,128)(2,1)}) custom-call(bf16[8,64,512]{2,1,0:T(8,128)(2,1)S(1)} %get-tuple-element.7.fine, s32[8,128]{1,0:T(8,128)S(1)} %get-tuple-element.8.keys, s32[8,128]{1,0:T(8,128)S(1)} %get-tuple-element.9.keys_in, bf16[2,128,256]{2,1,0:T(8,128)(2,1)S(1)} %get-tuple-element.10.octs, ...), custom_call_target="tpu_custom_call" | custom-call | tf_op jit(solution)/shard_map/finish/pallas_call | solution.py:415

commit v8 on v7

--- a/solution.py
+++ b/solution.py
@@ -98,7 +98,7 @@
     return jnp.concatenate(columns, axis=1)
 
 
-def place(keys, near, far, coarse, count):
+def place(keys, octants, coarse, count):
     k = lax.broadcasted_iota(jnp.int32, (64, 512), 0)
     lane = lax.broadcasted_iota(jnp.int32, (64, 512), 1)
     rest = lane - (64 * (k >> 4) + 8 * ((k >> 2) & 3) + (k & 3))
@@ -109,7 +109,6 @@
     blocks = [
         jnp.where(rest == starts[j : j + 1], 1.0, 0.0).astype(jnp.bfloat16) for j in range(count)
     ]
-    octants = jnp.concatenate([near, far], axis=1)
     return dot(octants, jnp.concatenate(blocks, axis=0))
 
 
@@ -231,11 +230,8 @@
     for a in range(3):
         weight_t[64 * a : 64 * a + 64] = flipped(weight[576 * a : 576 * a + 576])
 
-    def activate_rest(i, carry):
+    for i in range(count):
         activate(i, 128, 256)
-        return carry
-
-    lax.fori_loop(0, count, activate_rest, 0, unroll=4)
     y_low = (lane & 63) < 32
     z_low = (lane & 7) < 4
     marks = ((lane & 63) < 8, (lane & 63) >= 56)
@@ -291,55 +287,47 @@
         upper[2 * j] = fallen[j]
         upper[2 * j + 1] = turn(fallen[j], 64)
 
-    step = count // 2
     outside = jnp.concatenate([weight_t[0:64], weight_t[128:192]], axis=0)
-    sent = []
-    for g in range(2):
-        group = pl.ds(g * step, step)
-        tall = []
-        for n in range(step):
-            i = g * step + n
-
-            def outer(dy, dz):
-                return jnp.where(half, upper[row(i, 1, dy, dz)], lower[row(i, -1, dy, dz)])
-
-            tall.append((outer(0, 0), *halos(outer, y_low, z_low)))
-        stacked = stack(tall, marks, side[...])
-        product = dot(outside, stacked)
-        for n in range(step):
-            i = g * step + n
-            mine = product[:, 128 * n : 128 * n + 128]
-            turned = pltpu.roll(jnp.where(half, mine[64:], mine[:64]), 64, 1)
-            mask = occ_ref[pl.ds(i, 1), :].astype(jnp.float32)
-            summed = feat[i].astype(jnp.float32) + conv[i] + shift
-            ends = jnp.concatenate(
-                [
-                    jnp.where(half, turned, 0.0),
-                    jnp.zeros((64, 256), jnp.float32),
-                    jnp.where(half, 0.0, turned),
-                ],
-                axis=1,
-            )
-            fine[i] = (mask * (summed + ends)).astype(jnp.bfloat16)
-        ordered = dot(fine[group].reshape(step * 64, 512), perm[...])
-        columns = []
-        for j in range(0, step, 2):
-            taps = []
-            for s in range(4):
-                one = ordered[64 * j : 64 * j + 64, 128 * s : 128 * s + 128]
-                two = ordered[64 * j + 64 : 64 * j + 128, 128 * s : 128 * s + 128]
-                taps.append(jnp.where(half, one, pltpu.roll(two, 64, 1)))
-                taps.append(jnp.where(half, pltpu.roll(one, 64, 1), two))
-            columns.append(jnp.concatenate(taps, axis=0).astype(jnp.bfloat16))
-        octants = dot(stride_t, jnp.concatenate(columns, axis=1)) + bias
-        octs[g] = octants.astype(jnp.bfloat16)
-        swap = remote(3 + g, octs.at[g], octs_in.at[g], mate)
-        swap.start()
-        sent.append(swap)
+    tall = []
+    for i in range(count):
+
+        def outer(dy, dz):
+            return jnp.where(half, upper[row(i, 1, dy, dz)], lower[row(i, -1, dy, dz)])
+
+        tall.append((outer(0, 0), *halos(outer, y_low, z_low)))
+    stacked = stack(tall, marks, side[...])
+    product = dot(outside, stacked)
+    for i in range(count):
+        mine = product[:, 128 * i : 128 * i + 128]
+        turned = pltpu.roll(jnp.where(half, mine[64:], mine[:64]), 64, 1)
+        mask = occ_ref[pl.ds(i, 1), :].astype(jnp.float32)
+        summed = feat[i].astype(jnp.float32) + conv[i] + shift
+        ends = jnp.concatenate(
+            [
+                jnp.where(half, turned, 0.0),
+                jnp.zeros((64, 256), jnp.float32),
+                jnp.where(half, 0.0, turned),
+            ],
+            axis=1,
+        )
+        fine[i] = (mask * (summed + ends)).astype(jnp.bfloat16)
+    ordered = dot(fine[...].reshape(count * 64, 512), perm[...])
+    columns = []
+    for j in range(0, count, 2):
+        taps = []
+        for s in range(4):
+            one = ordered[64 * j : 64 * j + 64, 128 * s : 128 * s + 128]
+            two = ordered[64 * j + 64 : 64 * j + 128, 128 * s : 128 * s + 128]
+            taps.append(jnp.where(half, one, pltpu.roll(two, 64, 1)))
+            taps.append(jnp.where(half, pltpu.roll(one, 64, 1), two))
+        columns.append(jnp.concatenate(taps, axis=0).astype(jnp.bfloat16))
+    octants = dot(stride_t, jnp.concatenate(columns, axis=1)) + bias
+    octs[...] = octants.astype(jnp.bfloat16)
+    swap = remote(3, octs, octs_in, mate)
+    swap.start()
 
     swap_keys.wait()
-    for swap in sent:
-        swap.wait()
+    swap.wait()
 
 
 def finish(fine, keys, keys_in, octs, octs_in, fine_hbm, coarse_hbm, coarse, sem):
@@ -347,8 +335,8 @@
     device = lax.axis_index("bricks") * lax.axis_size("grp") + lax.axis_index("grp")
     store = pltpu.make_async_copy(fine, fine_hbm, sem.at[0])
     store.start()
-    total = place(keys[...], octs[0], octs[1], device, count)
-    total = total + place(keys_in[...], octs_in[0], octs_in[1], device, count)
+    total = place(keys[...], octs[...], device, count)
+    total = total + place(keys_in[...], octs_in[...], device, count)
     coarse[0] = total.astype(jnp.bfloat16)
     last = pltpu.make_async_copy(coarse, coarse_hbm, sem.at[1])
     last.start()
@@ -370,8 +358,8 @@
             jax.ShapeDtypeStruct(features.shape, bf16),
             jax.ShapeDtypeStruct((count, 128), jnp.int32),
             jax.ShapeDtypeStruct((count, 128), jnp.int32),
-            jax.ShapeDtypeStruct((2, 128, 32 * count), bf16),
-            jax.ShapeDtypeStruct((2, 128, 32 * count), bf16),
+            jax.ShapeDtypeStruct((128, 64 * count), bf16),
+            jax.ShapeDtypeStruct((128, 64 * count), bf16),
         ),
         in_specs=[hbm] * 11,
         out_specs=(vmem,) * 5,

time: 15 us -> 14.1 us (0.940)
  Pallas kernels: 14.1 us -> 13.3 us
    pallas_call x1, Pallas kernels: 13.1 us -> 12.3 us  [shards(): pl.pallas_call(kernel, out_shape=(jax.ShapeDtypeStruct(features.shape, bf...]
where the time goes in v8:
time: 14.1 us; the launch traced here: 13.9 us
  Pallas kernels  13.3 us (94%)
  between operations  0.64 us (5%)
    pallas_call x1, Pallas kernels, shards(): pl.pallas_call(kernel, out_shape=(jax.ShapeDtypeStruct(features.shape, bf...  12.3 us
    pallas_call x1, Pallas kernels, shards(): pl.pallas_call(finish, out_shape=(jax.ShapeDtypeStruct(features.shape, bf...  1 us

profile of v8, /device:TPU:5, one launch (start us, length us, event | category | flops | bytes accessed | tf_op | source)
XLA Modules:
  0.0 13.9 jit_solution(707605421477299216)
XLA Ops:
  0.6 12.3 %bricks.1 = (bf16[8,64,512]{2,1,0:T(8,128)(2,1)S(1)}, s32[8,128]{1,0:T(8,128)S(1)}, s32[8,128]{1,0:T(8,128)S(1)}, bf16[128,512]{1,0:T(8,128)(2,1)S(1)}, bf16[128,512]{1,0:T(8,128)(2,1)S(1)}) custom-call(s32[8,512]{1,0:T(8,128)} %occ_hbm.1, f32[1,64]{1,0:T(1,128)} %bitcast.8, bf16[8,64,512]{2,1,0:T(8,128)(2,1)} %feat_hbm.1, s32[1,8]{1,0:T(1,128)} %bitcast.9, ...), custom_call_target="tpu_custom_call" | custom-call | tf_op jit(solution)/shard_map/bricks/pallas_call | solution.py:355
  12.9 1.0 %finish.1 = (bf16[8,64,512]{2,1,0:T(8,128)(2,1)}, bf16[1,128,512]{2,1,0:T(8,128)(2,1)}) custom-call(bf16[8,64,512]{2,1,0:T(8,128)(2,1)S(1)} %get-tuple-element.7.fine, s32[8,128]{1,0:T(8,128)S(1)} %get-tuple-element.8.keys, s32[8,128]{1,0:T(8,128)S(1)} %get-tuple-element.9.keys_in, bf16[128,512]{1,0:T(8,128)(2,1)S(1)} %get-tuple-element.10.octs, ...), custom_call_target="tpu_custom_call" | custom-call | tf_op jit(solution)/shard_map/finish/pallas_call | solution.py:403

commit v9 on v8

--- a/solution.py
+++ b/solution.py
@@ -269,7 +269,7 @@
         conv[i] = jnp.concatenate(pieces, axis=1)
         return carry
 
-    lax.fori_loop(0, count, middle, 0, unroll=4)
+    lax.fori_loop(0, count, middle, 0, unroll=count)
 
     @pl.when(has_left)
     def _():

time: 14.1 us -> 13.6 us (0.965)
  Pallas kernels: 13.3 us -> 12.7 us
    pallas_call x1, Pallas kernels: 12.3 us -> 11.7 us  [shards(): pl.pallas_call(kernel, out_shape=(jax.ShapeDtypeStruct(features.shape, bf...]
where the time goes in v9:
time: 13.6 us; the launch traced here: 13.4 us
  Pallas kernels  12.7 us (93%)
  between operations  0.64 us (5%)
    pallas_call x1, Pallas kernels, shards(): pl.pallas_call(kernel, out_shape=(jax.ShapeDtypeStruct(features.shape, bf...  11.7 us
    pallas_call x1, Pallas kernels, shards(): pl.pallas_call(finish, out_shape=(jax.ShapeDtypeStruct(features.shape, bf...  1 us

profile of v9, /device:TPU:5, one launch (start us, length us, event | category | flops | bytes accessed | tf_op | source)
XLA Modules:
  0.0 13.4 jit_solution(6016951731640338671)
XLA Ops:
  0.6 11.7 %bricks.1 = (bf16[8,64,512]{2,1,0:T(8,128)(2,1)S(1)}, s32[8,128]{1,0:T(8,128)S(1)}, s32[8,128]{1,0:T(8,128)S(1)}, bf16[128,512]{1,0:T(8,128)(2,1)S(1)}, bf16[128,512]{1,0:T(8,128)(2,1)S(1)}) custom-call(s32[8,512]{1,0:T(8,128)} %occ_hbm.1, f32[1,64]{1,0:T(1,128)} %bitcast.8, bf16[8,64,512]{2,1,0:T(8,128)(2,1)} %feat_hbm.1, s32[1,8]{1,0:T(1,128)} %bitcast.9, ...), custom_call_target="tpu_custom_call" | custom-call | tf_op jit(solution)/shard_map/bricks/pallas_call | solution.py:355
  12.4 1.0 %finish.1 = (bf16[8,64,512]{2,1,0:T(8,128)(2,1)}, bf16[1,128,512]{2,1,0:T(8,128)(2,1)}) custom-call(bf16[8,64,512]{2,1,0:T(8,128)(2,1)S(1)} %get-tuple-element.7.fine, s32[8,128]{1,0:T(8,128)S(1)} %get-tuple-element.8.keys, s32[8,128]{1,0:T(8,128)S(1)} %get-tuple-element.9.keys_in, bf16[128,512]{1,0:T(8,128)(2,1)S(1)} %get-tuple-element.10.octs, ...), custom_call_target="tpu_custom_call" | custom-call | tf_op jit(solution)/shard_map/finish/pallas_call | solution.py:403
